TPU v7x, 128 devices: a whole 4x4x4 slice. The times are simulated.
128 devices in a mesh: face: 8 (over x_lo, y), tile: 16 (over x_hi, z, core).
Axes of the slice: x: 4 (x_hi: 2, x_lo: 2; x = x_hi * 2 + x_lo), y: 4, z: 4, core: 2. Of those that a mesh axis runs over, the one named last changes fastest.
Arguments:
- checkpoint: bfloat16 [48, 32768], P(None, 'tile'), may hold values from -6 to 6
- remap_weights: bfloat16 [8, 16, 16, 256, 1024], P('face', 'tile'), may hold values from -0.09375 to 0.09375
- margins: int32 [8, 16, 16], P('face', 'tile'), may hold values from 0 to 127, as said below
- seams: int32 [8, 16, 3, 4], P('face', 'tile'), may hold values from 0 to 127, as said below
- rotation_angle: float32 [8, 16, 1024], P('face', 'tile'), may hold values from -3.140625 to 3.140625
Outputs:
- scalars: bfloat16 [8, 16, 32, 1024], P('face', 'tile')
- dgrid_winds: bfloat16 [8, 16, 16, 1024], P('face', 'tile')
- vorticity: float32 [8, 16, 8, 1024], P('face', 'tile')
Inputs may be any that keep to these rules, and one draw needn't show every extreme that they name: `margins`: each tile lists 16 block ids in rising order; entries 2 m to 2 m + 1 lie in the blocks of one reader (id // 8), a different reader for each m, so every tile takes exactly 2 blocks from each of 8 readers. seams[f, g, 0, e] is the number f2 16 + g2 of the tile across edge e, seams[f, g, 1, e] the edge of that tile, seams[f, g, 2, e] is 1 where the two rims run opposite ways and 0 else; the pairing is symmetric with equal flags, and the four tiles across one tile's edges are four different tiles, none of them the tile itself.
All inputs are finite; a program needn't handle non-finite values.
Results may differ from a plain program's by a relative error of at most 0.001.
Values may be sent and summed in bfloat16 or wider, within the bound.
No kernel may reach another device: no remote copies, remote signals or barrier semaphores. Data moves between devices by JAX's collectives and lax.ppermute only.
A program may use at most 64 MiB of HBM per device.

v0:
```python
import jax
import jax.numpy as jnp
from jax import lax
from jax.sharding import PartitionSpec as P

LEV = 8
FIELDS = 6
TS = 32
SB = 256
K = 16
SMOOTH = 2


def edge_rims(grid_field):
    return jnp.stack(
        [grid_field[:, -1, :], grid_field[:, :, -1], grid_field[:, 0, :], grid_field[:, :, 0]],
        axis=0,
    )


def neighbours(gathered, seam_table):
    slot_index = seam_table[0] * 4 + seam_table[1]
    picked = jnp.take(gathered, slot_index, axis=0)
    return jnp.where((seam_table[2] == 1)[:, None, None], jnp.flip(picked, axis=-1), picked)


def shifted(grid_field, halo_rims):
    plus_x = jnp.concatenate([grid_field[:, :, 1:], halo_rims[1][:, :, None]], axis=2)
    minus_x = jnp.concatenate([halo_rims[3][:, :, None], grid_field[:, :, :-1]], axis=2)
    plus_y = jnp.concatenate([grid_field[:, 1:, :], halo_rims[0][:, None, :]], axis=1)
    minus_y = jnp.concatenate([halo_rims[2][:, None, :], grid_field[:, :-1, :]], axis=1)
    return (plus_x, minus_x, plus_y, minus_y)


def dgrid_and_curl(wind_field, plus_x, minus_x, plus_y, minus_y, angle):
    wind_levels = wind_field.shape[0] // 2
    cosine = jnp.cos(angle)
    sine_part = jnp.sin(angle)
    eastward = wind_field[:wind_levels]
    northward = wind_field[wind_levels:]
    along_edge = cosine * (0.5 * (eastward + plus_y[:wind_levels])) + sine_part * (
        0.5 * (northward + plus_y[wind_levels:])
    )
    across = -sine_part * (0.5 * (eastward + plus_x[:wind_levels])) + cosine * (
        0.5 * (northward + plus_x[wind_levels:])
    )
    curl_field = cosine * (
        0.5 * (plus_x[wind_levels:] - minus_x[wind_levels:])
        - 0.5 * (plus_y[:wind_levels] - minus_y[:wind_levels])
    )
    curl_field = curl_field - sine_part * (
        0.5 * (plus_x[:wind_levels] - minus_x[:wind_levels])
        + 0.5 * (plus_y[wind_levels:] - minus_y[wind_levels:])
    )
    return (jnp.concatenate([along_edge, across], axis=0), curl_field)


def wind_halos(wind_field, seam_table):
    wind_edges = lax.all_gather(edge_rims(wind_field), ("face", "tile"), axis=0, tiled=True)
    return shifted(wind_field, neighbours(wind_edges, seam_table))


def vortex_halos(vortex, seam_table):
    vort_edges = lax.all_gather(edge_rims(vortex), ("face", "tile"), axis=0, tiled=True)
    return shifted(vortex, neighbours(vort_edges, seam_table))


def body(checkpoint, remap_weights, margins, seams, rotation_angle):
    channels = checkpoint.shape[0]
    block_ids = margins[0, 0]
    empty = jnp.zeros((channels, K, SB), jnp.bfloat16)
    piece = lax.all_gather(checkpoint, "tile", axis=1, tiled=True)
    count_here = piece.shape[1] // SB
    inside = (block_ids >= 0) & (block_ids < count_here)
    picked_rows = jnp.take(
        piece.reshape(channels, count_here, SB), jnp.clip(block_ids, 0, count_here - 1), axis=1
    )
    chosen = jnp.where(inside[None, :, None], picked_rows, empty)
    weights = remap_weights[0, 0].reshape(K * SB, TS * TS)
    remapped = jnp.dot(
        chosen.reshape(channels, K * SB), weights, preferred_element_type=jnp.float32
    )
    scalars = remapped[2 * LEV :].astype(jnp.bfloat16)
    wind_field = remapped[: 2 * LEV].reshape(2 * LEV, TS, TS)
    seam_table = seams[0, 0]
    angle = rotation_angle[0, 0].reshape(TS, TS)
    wind_shifts = wind_halos(wind_field, seam_table)
    dgrid, vortex = dgrid_and_curl(
        wind_field, wind_shifts[0], wind_shifts[1], wind_shifts[2], wind_shifts[3], angle
    )
    for repeat in range(SMOOTH):
        vort_shifts = vortex_halos(vortex, seam_table)
        vortex = vortex + 0.2 * (
            vort_shifts[0] + vort_shifts[1] + vort_shifts[2] + vort_shifts[3] - 4.0 * vortex
        )
    scalars = scalars.reshape(1, 1, (FIELDS - 2) * LEV, TS * TS)
    dgrid = dgrid.astype(jnp.bfloat16).reshape(1, 1, 2 * LEV, TS * TS)
    vortex = vortex.reshape(1, 1, LEV, TS * TS)
    return (scalars, dgrid, vortex)


def solution(mesh):
    placed = (
        P(None, "tile"),
        P("face", "tile", None, None, None),
        P("face", "tile", None),
        P("face", "tile", None, None),
        P("face", "tile", None),
    )
    return jax.shard_map(
        body,
        mesh=mesh,
        in_specs=placed,
        out_specs=(
            P("face", "tile", None, None),
            P("face", "tile", None, None),
            P("face", "tile", None, None),
        ),
        check_vma=False,
    )
```

profile of v0, /device:TPU:1, one launch (start us, length us, event | category | flops | bytes accessed | tf_op | source)
XLA Modules:
  0.0 648.1 jit_solution(3661771317356172928)
XLA Ops:
  7.2 0.7 all-gather.3.cloned.1.call-update
  7.9 0.7 fusion.26
  8.6 1.2 compare_and_fusion.1
  9.8 1.2 and_bitcast_fusion
  11.0 1.2 compare_select_fusion.1
  12.1 0.8 fusion.39
  13.0 52.1 %all-gather.3.cloned.1.call-done = bf16[48,32768]{1,0:T(8,128)(2,1)} async-done(((bf16[48,2048]{1,0:T(8,128)(2,1)}), bf16[48,32768]{1,0:T(8,128)(2,1)}) %all-gather.3.cloned.1.call-update) | async-done | bytes 3145744 | tf_op jit(solution)/shard_map/all_gather | solution.py:72
  65.1 2.1 copy.147
  67.2 0.6 gather_fusion
  67.8 0.8 select_bitcast_fusion
  68.6 5.0 fusion.40
  74.2 0.6 pad_maximum_fusion.4
  75.1 0.7 mul.111
  75.7 0.6 pad_clamp_fusion
  76.3 0.7 compare_bitcast_fusion
  77.0 0.6 broadcast_multiply_fusion
  78.6 0.6 fusion.25
  79.3 191.6 %all-gather.5.cloned.1.call-done = f32[512,16,32]{2,1,0:T(8,128)} async-done(((f32[4,16,32]{2,1,0:T(8,128)}), f32[512,16,32]{2,1,0:T(8,128)}) %all-gather.5.cloned.1.call-update) | async-done | bytes 1048592 | tf_op jit(solution)/shard_map/all_gather | solution.py:59
  270.9 2.7 gather_fusion.1
  274.4 0.2 fusion.5
  274.6 0.7 fusion.36
  275.4 0.8 fusion.37
  276.4 180.4 %all_gather.14 = f32[512,8,32]{2,1,0:T(8,128)S(1)} all-gather(f32[4,8,32]{2,1,0:T(8,128)S(1)} %pad_maximum_fusion.6), channel_id=1, replica_groups=mesh['face'=8,'tile'=16] {'face','tile'}, dimensions={0}, use_global_device_ids=true | all-gather | bytes 528384 | tf_op jit(solution)/shard_map/all_gather | solution.py:64
  456.9 0.7 gather_fusion.2
  457.5 0.7 broadcast_select_fusion.3
  458.3 0.7 broadcast_select_fusion.5
  459.4 1.2 fusion.19
  460.9 1.0 add_convert_fusion.1
  462.4 176.1 %all_gather.15 = f32[512,8,32]{2,1,0:T(8,128)S(1)} all-gather(f32[4,8,32]{2,1,0:T(8,128)S(1)} %pad_maximum_fusion.7), channel_id=1, replica_groups=mesh['face'=8,'tile'=16] {'face','tile'}, dimensions={0}, use_global_device_ids=true | all-gather | bytes 528384 | tf_op jit(solution)/shard_map/all_gather | solution.py:64
  638.5 0.7 gather_fusion.3
  639.9 0.7 reshape.240
  640.6 0.6 pad_maximum_fusion.5
  (70 shorter events, 4.7 us)
Async XLA Ops:
  7.2 57.9 %all-gather.3.cloned.1.call-start = ((), (), s32[]{:S(2)}) async-start(), calls=%async_computation | async-start | bytes 3342336 | tf_op jit(solution)/shard_map/all_gather | solution.py:72
  7.9 263.0 %all-gather.5.cloned.1.call-start = ((), (), s32[]{:S(2)}) async-start(), calls=%async_computation.1 | async-start | bytes 4227072 | tf_op jit(solution)/shard_map/all_gather | solution.py:59
  68.6 7.7 %copy-start.4 = (s32[1,1,1,4]{3,1,2,0:T(1,128)S(1)}, s32[1,1,1,4]{3,1,2,0:T(1,128)}, u32[]{:S(2)}) copy-start(s32[1,1,1,4]{3,1,2,0:T(1,128)} %get-tuple-element.7) | copy-start | bytes 52
  77.0 197.1 %copy-start.2 = (pred[4]{0:T(512)(128)(4,1)}, pred[4]{0:T(512)(128)(4,1)S(1)}, u32[]{:S(2)}) copy-start(pred[4]{0:T(512)(128)(4,1)S(1)} %compare_bitcast_fusion) | copy-start | bytes 16
  77.0 197.1 %copy-start = (pred[4]{0:T(512)(128)(4,1)}, pred[4]{0:T(512)(128)(4,1)S(1)}, u32[]{:S(2)}) copy-start(pred[4]{0:T(512)(128)(4,1)S(1)} %compare_and_fusion) | copy-start | bytes 16
  460.6 178.6 %copy-start.1 = (pred[4]{0:T(512)(128)(4,1)S(1)}, pred[4]{0:T(512)(128)(4,1)}, u32[]{:S(2)}) copy-start(pred[4]{0:T(512)(128)(4,1)} %copy-done) | copy-start | bytes 16
  460.6 178.7 %copy-start.3 = (pred[4]{0:T(512)(128)(4,1)S(1)}, pred[4]{0:T(512)(128)(4,1)}, u32[]{:S(2)}) copy-start(pred[4]{0:T(512)(128)(4,1)} %copy-done.2) | copy-start | bytes 16
Sparse Core Ops, SparseCore 0:
  10.5 54.4 all-gather.2
  75.0 195.8 all-gather.4
where the time goes:
time: 649 us; the launch traced here: 648 us
  blocking collectives  357 us (55%)
  waiting for transfers between devices  244 us (38%)
  local copies, waits for them, and re-layouts  15.2 us (2%)
  between operations  14.4 us (2%)
  other arithmetic  12.5 us (2%)
    all_gather x2, blocking collectives, vortex_halos(): lax.all_gather(edge_rims(vortex), ('face', 'tile'), axis=0, tiled=True)  357 us
    all_gather x1, waiting for transfers between devices, wind_halos(): lax.all_gather(edge_rims(wind_field), ('face', 'tile'), axis=0, tiled=True)  192 us
    all_gather x1, waiting for transfers between devices, body(): piece = lax.all_gather(checkpoint, 'tile', axis=1, tiled=True)  52.1 us
  transfers between devices with their start and end apart: 2, of which 2 were waited for; matrix products, arithmetic and copies ran while one was open for 1% of the time, Pallas kernels for 0%

commit v1 on v0

v1 whole, which is shorter than its diff:
```python
import jax
import jax.numpy as jnp
from jax import lax
from jax.experimental import pallas as pl
from jax.experimental.pallas import tpu as pltpu
from jax.sharding import PartitionSpec as P

LEV = 8
FIELDS = 6
TS = 32
CELLS = TS * TS
SB = 256
BLK_DEV = 8
K = 16
CAP = 2
GROUPS = K // CAP
N_TILE = 16
TILES = 128
ROWS = FIELDS * LEV
WINDS = 2 * LEV
LANES = 128
MIB = 1 << 20
HEAD = 1024
CHUNK = 512
F32 = jnp.float32
BF16 = jnp.bfloat16


def iota(shape, dim):
    return lax.broadcasted_iota(jnp.int32, shape, dim)


def dot(a, b, contract=((1,), (0,))):
    return lax.dot_general(a, b, (contract, ((), ())), preferred_element_type=F32)


def halves(x):
    hi = x.astype(BF16).astype(F32)
    return hi, x - hi


def roll(x, shift):
    return pltpu.roll(x, shift % x.shape[1], 1)


def lane_pick(group, values):
    out = jnp.full(group.shape, values[0])
    for index in range(1, len(values)):
        out = jnp.where(group == index, values[index], out)
    return out


def towards(direction, cosine, sine, d_east, d_north):
    a_east = jnp.where(
        direction == 0, -cosine, jnp.where(direction == 1, -sine, jnp.where(direction == 2, cosine, sine))
    )
    a_north = jnp.where(
        direction == 0, -sine, jnp.where(direction == 1, cosine, jnp.where(direction == 2, sine, -cosine))
    )
    return 0.5 * (a_east * d_east + a_north * d_north)


def neighbours_within(h, row, col):
    return (
        jnp.where(col == TS - 1, h, roll(h, -1)),
        jnp.where(col == 0, h, roll(h, 1)),
        jnp.where(row == TS - 1, h, roll(h, -TS)),
        jnp.where(row == 0, h, roll(h, TS)),
    )


def ask_kernel(margins_ref, out_ref, margins, sem):
    copy = pltpu.make_async_copy(margins_ref, margins, sem)
    copy.start()
    copy.wait()
    reader, lane = iota((N_TILE, LANES), 0), iota((N_TILE, LANES), 1)
    asked = jnp.zeros((N_TILE, LANES), jnp.int32)
    for m in range(GROUPS):
        first, second = margins[CAP * m], margins[CAP * m + 1]
        asked = jnp.where(reader == (first >> 3), jnp.where(lane == 0, first, second), asked)
    asked = asked & (BLK_DEV - 1)
    for r in range(N_TILE):
        out_ref[r] = asked[r : r + 1]


def prepare_kernel(
    margins_ref, seams_ref, held_ref, meta_ref, held_out, sem
):
    copy = pltpu.make_async_copy(held_ref, held_out, sem)
    copy.start()

    level, lane = iota((LEV, LANES), 0), iota((LEV, LANES), 1)
    meta = jnp.zeros((LEV, LANES), jnp.int32)
    for m in range(GROUPS):
        reader = jnp.clip(margins_ref[CAP * m] >> 3, 0, N_TILE - 1)
        meta = jnp.where((level == 0) & (lane == m), reader, meta)
    for kind in range(3):
        for e in range(4):
            meta = jnp.where((level == kind + 1) & (lane == e), seams_ref[kind, e], meta)
    meta_ref[...] = meta
    copy.wait()


def select_kernel(asked_ref, held_ref, out_ref, sem):
    copies = []
    for g in range(N_TILE):
        for j in range(CAP):
            block = asked_ref[g, j] & (BLK_DEV - 1)
            copies.append(
                pltpu.make_async_copy(
                    held_ref.at[:, pl.ds(pl.multiple_of(block * SB, SB), SB)],
                    out_ref.at[g, :, pl.ds(j * SB, SB)],
                    sem.at[g, j],
                )
            )
    for copy in copies:
        copy.start()
    for copy in copies:
        copy.wait()


def fetch_kernel(weights_ref, asked_ref, head_ref, sem):
    copy = pltpu.make_async_copy(weights_ref.at[pl.ds(0, HEAD)], head_ref, sem)
    copy.start()
    copy.wait()


def remap_kernel(
    meta_ref, blocks_ref, head_ref, weights_ref, angle_ref,
    scalars_ref, wind_ref, trig_ref, place_ref, send_ref,
    chosen, streamed, pick_ref, scalars_out, sems, out_sem,
):
    spans = [(k, pl.ds(k, CHUNK)) for k in range(HEAD, K * SB, CHUNK)]
    copies = [
        pltpu.make_async_copy(weights_ref.at[span], streamed.at[pl.ds(k - HEAD, CHUNK)], sems.at[index])
        for index, (k, span) in enumerate(spans)
    ]
    for copy in copies:
        copy.start()
    for m in range(GROUPS):
        chosen[:, CAP * SB * m : CAP * SB * (m + 1)] = blocks_ref[meta_ref[0, m]]
    total = dot(chosen[:, :HEAD], head_ref[...])

    angle = angle_ref[...]
    trig_ref[...] = jnp.where((iota((LEV, CELLS), 0) & 1) == 0, jnp.cos(angle), jnp.sin(angle))

    lane = iota((1, 3 * LANES), 1)
    edge, depth, at = (lane >> 6) & 3, (lane >> 5) & 1, lane & 31
    rim_cell = jnp.where(
        edge == 0, (TS - 1 - depth) * TS + at,
        jnp.where(edge == 1, at * TS + TS - 1 - depth, jnp.where(edge == 2, depth * TS + at, at * TS + depth)),
    )
    corner, k = (lane >> 2) & 3, lane & 3
    c_row, c_col = (corner >> 1) * (TS - 1), (corner & 1) * (TS - 1)
    c_row = jnp.where(k == 2, jnp.where(c_row == 0, 1, TS - 2), c_row)
    c_col = jnp.where(k == 1, jnp.where(c_col == 0, 1, TS - 2), c_col)
    corner_cell = jnp.where((lane & 127) >= 96, c_row * TS + c_col, -1)
    taken = jnp.where(lane < 2 * LANES, rim_cell, corner_cell)
    pick_ref[...] = (iota((CELLS, 3 * LANES), 0) == taken).astype(F32).astype(BF16)

    line = iota((LANES, 1), 0)
    line_edge, line_at = line >> 5, line & 31
    flipped = lane_pick(line_edge, [meta_ref[3, e] for e in range(4)]) == 1
    line_at = jnp.where(flipped, TS - 1 - line_at, line_at)
    rim_cell = jnp.where(
        line_edge == 0, (TS - 1) * TS + line_at,
        jnp.where(line_edge == 1, line_at * TS + TS - 1, jnp.where(line_edge == 2, line_at, line_at * TS)),
    )
    place_ref[...] = (iota((LANES, CELLS), 1) == rim_cell).astype(F32).astype(BF16)

    for copy, (k, _) in zip(copies, spans):
        copy.wait()
        total = total + dot(chosen[:, k : k + CHUNK], streamed[k - HEAD : k - HEAD + CHUNK])
    scalars_out[...] = total[WINDS:].astype(BF16)
    out_copy = pltpu.make_async_copy(scalars_out, scalars_ref, out_sem)
    out_copy.start()
    wind = total[:WINDS]
    wind_ref[...] = wind
    east, north = wind[:LEV], wind[LEV:]

    cell = iota((1, CELLS), 1)
    row, col = cell >> 5, cell & (TS - 1)
    trig = trig_ref[...]
    cosine, sine = trig[0:1], trig[1:2]
    ex, exm, ey, eym = neighbours_within(east, row, col)
    nx, nxm, ny, nym = neighbours_within(north, row, col)
    curl = cosine * (0.5 * (nx - nxm) - 0.5 * (ey - eym)) - sine * (0.5 * (ex - exm) + 0.5 * (ny - nym))

    hi, lo = halves(jnp.concatenate([east, north, curl, trig], axis=0))
    got = dot(jnp.concatenate([hi, lo], axis=0).astype(BF16), pick_ref[...])

    lane = iota((LEV, LANES), 1)
    level = iota((LEV, LANES), 0)
    group = lane >> 5
    corners = got[:, 2 * LANES :]
    common_top = jnp.where((level == 5) | (level == 6), corners[24:32], 0.0)
    for e in range(4):
        tile = meta_ref[1, e].astype(F32)
        code = (meta_ref[2, e] * 2 + meta_ref[3, e]).astype(F32)
        common_top = jnp.where((level == 4) & (lane == 96 + e), tile, common_top)
        common_top = jnp.where((level == 4) & (lane == 100 + e), code, common_top)
    common_low = jnp.where(
        lane >= 112, corners[8:16], jnp.where((lane & 3) == 3, corners[16:24], corners[0:8])
    )
    common_low = jnp.where(group == 3, common_low, 0.0)
    common = jnp.concatenate([common_top, common_low], axis=0).astype(BF16)
    for t in range(TILES):
        send_ref[t] = common
    for e in range(4):
        rim = roll(got[:, LANES * (e // 2) : LANES * (e // 2 + 1)], -64 * (e % 2))
        top = jnp.where(
            group == 0, rim[0:8],
            jnp.where(group == 1, roll(rim[32:40], 32), jnp.where(group == 2, roll(rim[16:24], 64), common_top)),
        )
        top = jnp.where((group == 3) & (level < 2), roll(rim[24:32], 96), top)
        top = jnp.where((group == 3) & ((level == 2) | (level == 3)), roll(rim[24:32], 64), top)
        low = jnp.where(
            group == 0, rim[8:16],
            jnp.where(group == 1, roll(rim[40:48], 32), jnp.where(group == 2, roll(rim[16:24], 32), common_low)),
        )
        send_ref[jnp.clip(meta_ref[1, e], 0, TILES - 1)] = jnp.concatenate([top, low], axis=0).astype(BF16)
    out_copy.wait()


def smooth_kernel(
    meta_ref, packets_ref, wind_ref, trig_ref, place_ref, dgrid_ref, vortex_ref,
):
    def packet(tile):
        both = packets_ref[tile].astype(F32)
        return both[:LEV], both[LEV:]

    def corner_of(edge, end):
        return jnp.where((edge & 1) == 0, jnp.where(edge == 0, 2, 0) + end, 2 * end + jnp.where(edge == 1, 1, 0))

    lane = iota((LEV, LANES), 1)
    level = iota((LEV, LANES), 0)
    group = lane >> 5
    at = lane & 31
    zero = jnp.zeros((LEV, LANES), F32)
    edges = [meta_ref[2, e] for e in range(4)]
    near = [packet(jnp.clip(meta_ref[1, e], 0, TILES - 1)) for e in range(4)]

    def strip(half, source):
        out = roll(near[0][half], -32 * source)
        for e in range(1, 4):
            out = jnp.where(group == e, roll(near[e][half], 32 * (e - source)), out)
        return out

    east_hi, east_lo, c0, misc = [strip(0, s) for s in range(4)]
    north_hi, north_lo, c1 = [strip(1, s) for s in range(3)]
    east0, north0 = east_hi + east_lo, north_hi + north_lo
    cos0, sin0, cos1, sin1 = [misc[r : r + 1] for r in range(4)]
    lane1 = iota((1, LANES), 1)
    edge_of = lane_pick(lane1 >> 5, edges)

    far_e, far_n, far_qe, far_qn, far_c, far_cos, far_sin = (zero,) * 7
    own_qe, own_qn, last_e, last_n = (zero,) * 4
    side_v = jnp.zeros((1, LANES), jnp.int32)
    far_edge_v, far_side_v = side_v, side_v

    def code_at(top, e):
        codes = top * 8.0 + roll(top, -4)
        return jnp.sum(jnp.where((level == 4) & (lane == 96 + e), codes, 0.0)).astype(jnp.int32)

    for e in range(4):
        for end in range(2):
            here = lane == 32 * e + 31 * end
            here1 = lane1 == 32 * e + 31 * end
            goal = 32 * e + 31 * end + LANES

            def take(into, vector, source):
                return jnp.where(here, pltpu.roll(vector, (goal - source) & 127, 1), into)

            even = (edges[e] & 1) == 0
            side = jnp.where(even, 1 if end else 3, 0 if end else 2)
            high = (edges[e] < 2).astype(jnp.int32)
            c2 = corner_of(edges[e], end)
            q2 = jnp.where(even, 2, 1)
            own_qe = take(own_qe, near[e][1], 96 + 4 * c2 + q2)
            own_qn = take(own_qn, near[e][1], 112 + 4 * c2 + q2)
            code = code_at(near[e][0], side)
            far_edge, far_flip = (code >> 1) & 3, code & 1
            far_top, far_low = packet(jnp.clip(code >> 3, 0, TILES - 1))
            end3 = high ^ far_flip
            c3 = corner_of(far_edge, end3)
            q3 = jnp.where((far_edge & 1) == 0, 1, 2)
            far_e = take(far_e, far_low, 96 + 4 * c3)
            far_n = take(far_n, far_low, 112 + 4 * c3)
            far_qe = take(far_qe, far_low, 96 + 4 * c3 + q3)
            far_qn = take(far_qn, far_low, 112 + 4 * c3 + q3)
            far_c = take(far_c, far_low, 96 + 4 * c3 + 3)
            far_trig = take(zero, far_top, 96 + 4 * c3)
            far_cos, far_sin = far_cos + far_trig[6:7], far_sin + far_trig[5:6]
            far_side = jnp.where(
                (far_edge & 1) == 0, jnp.where(end3 == 1, 1, 3), jnp.where(end3 == 1, 0, 2)
            )
            code = code_at(far_top, far_side)
            last_edge, last_flip = (code >> 1) & 3, code & 1
            _, last_low = packet(jnp.clip(code >> 3, 0, TILES - 1))
            c4 = corner_of(last_edge, (far_edge < 2).astype(jnp.int32) ^ last_flip)
            last_e = take(last_e, last_low, 96 + 4 * c4)
            last_n = take(last_n, last_low, 112 + 4 * c4)
            side_v = jnp.where(here1, side, side_v)
            far_edge_v = jnp.where(here1, far_edge, far_edge_v)
            far_side_v = jnp.where(here1, far_side, far_side_v)

    place = place_ref[...]
    cell = iota((1, CELLS), 1)
    row, col = cell >> 5, cell & (TS - 1)
    along_x = (group & 1) == 1

    def rims_of(fields):
        hi, lo = halves(fields)
        got = dot(jnp.concatenate([hi, lo], axis=0).astype(BF16), place, ((1,), (1,)))
        return got[: fields.shape[0]] + got[fields.shape[0] :]

    def placed(pairs):
        parts = [p for pair in pairs for p in pair]
        parts = [jnp.where(along_x, p, 0.0) for p in parts] + [jnp.where(along_x, 0.0, p) for p in parts]
        got = dot(jnp.concatenate(parts, axis=0).astype(BF16), place)
        got = [got[LEV * i : LEV * (i + 1)] for i in range(len(parts))]
        got = [got[i] + got[i + 1] for i in range(0, len(got), 2)]
        return [(got[i], got[i + len(pairs)]) for i in range(len(pairs))]

    def shifts(h, halo):
        halo_x, halo_y = halo
        return (
            jnp.where(col == TS - 1, halo_x, roll(h, -1)),
            jnp.where(col == 0, halo_x, roll(h, 1)),
            jnp.where(row == TS - 1, halo_y, roll(h, -TS)),
            jnp.where(row == 0, halo_y, roll(h, TS)),
        )

    wind = wind_ref[...]
    east, north = wind[:LEV], wind[LEV:]
    cosine, sine = trig_ref[0:1, :], trig_ref[1:2, :]
    rim = rims_of(wind)
    rim_e, rim_n = rim[:LEV], rim[LEV:]
    halo_e, halo_n = placed([(east_hi, east_lo), (north_hi, north_lo)])
    ex, exm, ey, eym = shifts(east, halo_e)
    nx, nxm, ny, nym = shifts(north, halo_n)
    along = cosine * (0.5 * (east + ey)) + sine * (0.5 * (north + ny))
    across = -sine * (0.5 * (east + ex)) + cosine * (0.5 * (north + nx))
    dgrid_ref[...] = jnp.concatenate([along, across], axis=0).astype(BF16)
    vortex = cosine * (0.5 * (nx - nxm) - 0.5 * (ey - eym)) - sine * (0.5 * (ex - exm) + 0.5 * (ny - nym))

    c0 = c0 + towards(edge_of, cos0, sin0, rim_e - east0, rim_n - north0)
    ends = (at == 0) | (at == 31)
    c0 = c0 + jnp.where(ends, towards(side_v, cos0, sin0, far_e - east0, far_n - north0), 0.0)
    c1 = c1 + jnp.where(ends, towards(side_v, cos1, sin1, far_qe - own_qe, far_qn - own_qn), 0.0)
    far_c = far_c + towards(far_edge_v, far_cos, far_sin, east0 - far_e, north0 - far_n)
    far_c = far_c + towards(far_side_v, far_cos, far_sin, last_e - far_e, last_n - far_n)

    rim_c = rims_of(vortex)
    after = jnp.where(at == 31, far_c, roll(c0, -1))
    before = jnp.where(at == 0, far_c, roll(c0, 1))
    s0 = c0 + 0.2 * (c1 + rim_c + after + before - 4.0 * c0)
    halo_c, halo_s = placed([halves(c0), halves(s0)])
    for halo in (halo_c, halo_s):
        xp, xm, yp, ym = shifts(vortex, halo)
        vortex = vortex + 0.2 * (xp + xm + yp + ym - 4.0 * vortex)
    vortex_ref[...] = vortex


def vmem():
    return pl.BlockSpec(memory_space=pltpu.VMEM)


def smem():
    return pl.BlockSpec(memory_space=pltpu.SMEM)


def shape(dims, kind):
    return jax.ShapeDtypeStruct(dims, kind)


def anywhere():
    return pl.BlockSpec(memory_space=pl.ANY)


def hbm():
    return pl.BlockSpec(memory_space=pltpu.HBM)


def cost(flops, moved):
    return pl.CostEstimate(flops=flops, bytes_accessed=moved, transcendentals=0)


def body(checkpoint, remap_weights, margins, seams, rotation_angle):
    own_margins = margins[0, 0]
    weights = remap_weights[0, 0].reshape(K * SB, CELLS)
    limit = pltpu.CompilerParams(vmem_limit_bytes=16 * MIB)

    asked = pl.pallas_call(
        ask_kernel,
        out_shape=shape((N_TILE, 1, LANES), jnp.int32),
        in_specs=[hbm()],
        out_specs=vmem(),
        scratch_shapes=[pltpu.SMEM((K,), jnp.int32), pltpu.SemaphoreType.DMA],
        name="ask",
    )(own_margins)
    asked = lax.all_to_all(asked, "tile", 0, 0, tiled=True).reshape(N_TILE, LANES)

    meta, held = pl.pallas_call(
        prepare_kernel,
        out_shape=(shape((LEV, LANES), jnp.int32), shape(checkpoint.shape, BF16)),
        in_specs=[smem(), smem(), hbm()],
        out_specs=(vmem(),) * 2,
        scratch_shapes=[pltpu.SemaphoreType.DMA],
        compiler_params=limit,
        cost_estimate=cost(1 << 20, MIB),
        name="prepare",
    )(own_margins, seams[0, 0], checkpoint)
    blocks = pl.pallas_call(
        select_kernel,
        out_shape=shape((N_TILE, ROWS, CAP * SB), BF16),
        in_specs=[smem(), vmem()],
        out_specs=anywhere(),
        scratch_shapes=[pltpu.SemaphoreType.DMA((N_TILE, CAP))],
        compiler_params=limit,
        name="select",
    )(asked, held)
    blocks = lax.all_to_all(blocks, "tile", 0, 0, tiled=True)

    weights = pltpu.with_memory_space_constraint(weights, pltpu.HBM)
    head = pl.pallas_call(
        fetch_kernel,
        out_shape=shape((HEAD, CELLS), BF16),
        in_specs=[hbm(), anywhere()],
        out_specs=vmem(),
        scratch_shapes=[pltpu.SemaphoreType.DMA],
        compiler_params=limit,
        cost_estimate=cost(1 << 20, 4 * MIB),
        name="fetch",
    )(weights, asked)

    scalars, wind, trig, place, packets = pl.pallas_call(
        remap_kernel,
        out_shape=(
            shape((ROWS - WINDS, CELLS), BF16),
            shape((WINDS, CELLS), F32),
            shape((LEV, CELLS), F32),
            shape((LANES, CELLS), BF16),
            shape((TILES, 16, LANES), BF16),
        ),
        in_specs=[smem(), vmem(), vmem(), hbm(), vmem()],
        out_specs=(anywhere(),) + (vmem(),) * 4,
        scratch_shapes=[
            pltpu.VMEM((ROWS, K * SB), BF16),
            pltpu.VMEM((K * SB - HEAD, CELLS), BF16),
            pltpu.VMEM((CELLS, 3 * LANES), BF16),
            pltpu.VMEM((ROWS - WINDS, CELLS), BF16),
            pltpu.SemaphoreType.DMA(((K * SB - HEAD) // CHUNK,)),
            pltpu.SemaphoreType.DMA,
        ],
        compiler_params=limit,
        cost_estimate=cost(2 * ROWS * K * SB * CELLS, 9 * MIB),
        name="remap",
    )(meta, blocks, head, weights, rotation_angle[0, 0].reshape(1, CELLS))
    packets = lax.all_to_all(packets, ("face", "tile"), 0, 0, tiled=True)

    dgrid, vortex = pl.pallas_call(
        smooth_kernel,
        out_shape=(shape((WINDS, CELLS), BF16), shape((LEV, CELLS), F32)),
        in_specs=[smem()] + [vmem()] * 4,
        out_specs=(vmem(), vmem()),
        compiler_params=limit,
        name="smooth",
    )(meta, packets, wind, trig, place)
    return (
        scalars.reshape(1, 1, ROWS - WINDS, CELLS),
        dgrid.reshape(1, 1, WINDS, CELLS),
        vortex.reshape(1, 1, LEV, CELLS),
    )


def solution(mesh):
    placed = (
        P(None, "tile"),
        P("face", "tile", None, None, None),
        P("face", "tile", None),
        P("face", "tile", None, None),
        P("face", "tile", None),
    )
    return jax.shard_map(
        body,
        mesh=mesh,
        in_specs=placed,
        out_specs=(P("face", "tile", None, None),) * 3,
        check_vma=False,
    )
```

time: 649 us -> 66.4 us (0.10)
  blocking collectives: 357 us -> 19.4 us
  waiting for transfers between devices: 244 us -> 16.7 us
  between operations: 14.4 us -> 0.68 us
  Pallas kernels: 0 us -> 13.6 us
  starting transfers between devices: 0.08 us -> 13.4 us
  local copies, waits for them, and re-layouts: 15.2 us -> 2.27 us
  other arithmetic: 12.5 us -> 0 us
    all_gather x2 -> x0, blocking collectives: 357 us -> none  [vortex_halos(): lax.all_gather(edge_rims(vortex), ('face', 'tile'), axis=0, tiled=True)]
    all_gather x2 -> x0, waiting for transfers between devices: 244 us -> none  [the longest x1 192 us: wind_halos(): lax.all_gather(edge_rims(wind_field), ('face', 'tile'), axis=0, tiled=True)]
    all_to_all x0 -> x1, blocking collectives: none -> 19.4 us  [body(): packets = lax.all_to_all(packets, ('face', 'tile'), 0, 0, tiled=True)]
    all_to_all x0 -> x2, waiting for transfers between devices: none -> 16.7 us  [the longest x1 12.9 us: body(): blocks = lax.all_to_all(blocks, 'tile', 0, 0, tiled=True)]
    pallas_call x0 -> x6, Pallas kernels: none -> 13.6 us  [the longest x1 4.6 us: body(): pl.pallas_call(remap_kernel, out_shape=(shape((ROWS - WINDS, CELLS), BF16...]
    all_to_all x0 -> x2, starting transfers between devices: none -> 13.4 us  [the longest x1 9.3 us: body(): lax.all_to_all(asked, 'tile', 0, 0, tiled=True).reshape(N_TILE, LANES)]
  transfers between devices with their start and end apart: 2 -> 2, of which waited for: 2 -> 2; matrix products, arithmetic and copies ran while one was open for 1% -> 1% of each run, Pallas kernels for 0% -> 4%
where the time goes in v1:
time: 66.4 us; the launch traced here: 66 us
  blocking collectives  19.4 us (29%)
  waiting for transfers between devices  16.7 us (25%)
  Pallas kernels  13.6 us (20%)
  starting transfers between devices  13.4 us (20%)
  local copies, waits for them, and re-layouts  2.27 us (3%)
  between operations  0.68 us (1%)
    all_to_all x1, blocking collectives, body(): packets = lax.all_to_all(packets, ('face', 'tile'), 0, 0, tiled=True)  19.4 us
    all_to_all x1, waiting for transfers between devices, body(): blocks = lax.all_to_all(blocks, 'tile', 0, 0, tiled=True)  12.9 us
    all_to_all x1, starting transfers between devices, body(): lax.all_to_all(asked, 'tile', 0, 0, tiled=True).reshape(N_TILE, LANES)  9.3 us
    pallas_call x1, Pallas kernels, body(): pl.pallas_call(remap_kernel, out_shape=(shape((ROWS - WINDS, CELLS), BF16...  4.6 us
    all_to_all x1, starting transfers between devices, body(): blocks = lax.all_to_all(blocks, 'tile', 0, 0, tiled=True)  4.08 us
    all_to_all x1, waiting for transfers between devices, body(): lax.all_to_all(asked, 'tile', 0, 0, tiled=True).reshape(N_TILE, LANES)  3.78 us
    pallas_call x1, Pallas kernels, body(): pl.pallas_call(smooth_kernel, out_shape=(shape((WINDS, CELLS), BF16), sha...  3.33 us
    unnamed x7, local copies, waits for them, and re-layouts  2.27 us
  transfers between devices with their start and end apart: 2, of which 2 were waited for; matrix products, arithmetic and copies ran while one was open for 1% of the time, Pallas kernels for 4%

profile of v1, /device:TPU:1, one launch (start us, length us, event | category | flops | bytes accessed | tf_op | source)
XLA Modules:
  0.0 66.0 jit_solution(9137621122143287085)
XLA Ops:
  0.6 0.0 copy-start.1
  0.6 1.4 %ask.1 = s32[16,1,128]{2,1,0:T(1,128)} custom-call(s32[16]{0:T(128)} %bitcast.14), custom_call_target="tpu_custom_call" | custom-call | tf_op jit(solution)/shard_map/ask/pallas_call | solution.py:394
  2.1 9.3 %all-to-all-start = ((s32[16,1,128]{2,1,0:T(1,128)}), s32[16,1,128]{2,1,0:T(1,128)S(1)}, u32[]{:S(2)}, u32[]{:S(2)}) async-start(s32[16,1,128]{2,1,0:T(1,128)} %ask.1), calls=%async_computation | async-start | bytes 16384 | tf_op jit(solution)/shard_map/all_to_all | solution.py:402
  11.4 0.7 %copy.11 = s32[1,1,3,4]{3,2,1,0:T(4,128)S(1)} copy(s32[1,1,3,4]{3,1,2,0:T(1,128)} %param.8) | data formatting | bytes 96
  12.0 0.0 copy-start
  12.1 0.9 %copy-done = bf16[48,2048]{1,0:T(8,128)(2,1)S(1)} copy-done((bf16[48,2048]{1,0:T(8,128)(2,1)S(1)}, bf16[48,2048]{1,0:T(8,128)(2,1)}, u32[]{:S(2)}) %copy-start) | copy-done | bytes 196632
  13.0 0.0 copy-start.2
  13.0 0.7 copy-done.2
  13.6 0.9 %prepare.1 = (s32[8,128]{1,0:T(8,128)S(1)}, bf16[48,2048]{1,0:T(8,128)(2,1)S(1)}) custom-call(s32[16]{0:T(128)S(1)} %bitcast.15, s32[3,4]{1,0:T(4,128)S(1)} %bitcast.12, bf16[48,2048]{1,0:T(8,128)(2,1)S(1)} %copy-done), custom_call_target="tpu_custom_call" | custom-call | flops 1048576 | bytes 1048576 | tf_op jit(solution)/shard_map/prepare/pallas_call | solution.py:404
  14.5 3.8 %all-to-all-done = s32[16,1,128]{2,1,0:T(1,128)S(1)} async-done(((s32[16,1,128]{2,1,0:T(1,128)}), s32[16,1,128]{2,1,0:T(1,128)S(1)}, u32[]{:S(2)}, u32[]{:S(2)}) %all-to-all-start) | async-done | bytes 8224 | tf_op jit(solution)/shard_map/all_to_all | solution.py:402
  18.3 1.8 %select.1 = bf16[16,48,512]{2,1,0:T(8,128)(2,1)} custom-call(s32[16,128]{1,0:T(8,128)S(1)} %bitcast.10, bf16[48,2048]{1,0:T(8,128)(2,1)S(1)} %get-tuple-element.13.held_ref), custom_call_target="tpu_custom_call" | custom-call | tf_op jit(solution)/shard_map/select/pallas_call | solution.py:414
  20.1 4.1 %all-to-all-start.1 = ((bf16[16,48,512]{2,1,0:T(8,128)(2,1)}), bf16[16,48,512]{2,1,0:T(8,128)(2,1)S(1)}, u32[]{:S(2)}, u32[]{:S(2)}) async-start(bf16[16,48,512]{2,1,0:T(8,128)(2,1)} %select.1), calls=%async_computation.1 | async-start | bytes 1572864 | tf_op jit(solution)/shard_map/all_to_all | solution.py:423
  24.2 1.6 %fetch.1.head_ref = bf16[1024,1024]{1,0:T(8,128)(2,1)S(1)} custom-call(bf16[4096,1024]{1,0:T(8,128)(2,1)} %bitcast.16, s32[16,128]{1,0:T(8,128)S(1)} %bitcast.11), custom_call_target="tpu_custom_call" | custom-call | flops 1048576 | bytes 4194304 | tf_op jit(solution)/shard_map/fetch/pallas_call | solution.py:426
  25.8 12.9 %all-to-all-done.1.blocks_ref = bf16[16,48,512]{2,1,0:T(8,128)(2,1)S(1)} async-done(((bf16[16,48,512]{2,1,0:T(8,128)(2,1)}), bf16[16,48,512]{2,1,0:T(8,128)(2,1)S(1)}, u32[]{:S(2)}, u32[]{:S(2)}) %all-to-all-start.1) | async-done | bytes 786464 | tf_op jit(solution)/shard_map/all_to_all | solution.py:423
  38.7 0.0 copy-done.1
  38.7 4.6 %remap.1 = (bf16[32,1024]{1,0:T(8,128)(2,1)}, f32[16,1024]{1,0:T(8,128)S(1)}, f32[8,1024]{1,0:T(8,128)S(1)}, bf16[128,1024]{1,0:T(8,128)(2,1)S(1)}, bf16[128,16,128]{2,1,0:T(8,128)(2,1)S(1)}) custom-call(s32[8,128]{1,0:T(8,128)S(1)} %get-tuple-element.12.meta_ref, bf16[16,48,512]{2,1,0:T(8,128)(2,1)S(1)} %all-to-all-done.1.blocks_ref, ...), custom_call_target="tpu_custom_call" | custom-call | flops 402653184 | bytes 9437184 | tf_op jit(solution)/shard_map/remap/pallas_call | solution.py:437
  43.3 19.4 %all_to_all.15.packets_ref = bf16[128,16,128]{2,1,0:T(8,128)(2,1)S(1)} all-to-all(bf16[128,16,128]{2,1,0:T(8,128)(2,1)S(1)} %get-tuple-element.15), channel_id=1, replica_groups=mesh['face'=8,'tile'=16] {'face','tile'}, dimensions={0} | all-to-all | bytes 1048576 | tf_op jit(solution)/shard_map/all_to_all | solution.py:460
  62.7 3.3 %smooth.1 = (bf16[16,1024]{1,0:T(8,128)(2,1)}, f32[8,1024]{1,0:T(8,128)}) custom-call(s32[8,128]{1,0:T(8,128)S(1)} %get-tuple-element.12.meta_ref, bf16[128,16,128]{2,1,0:T(8,128)(2,1)S(1)} %all_to_all.15.packets_ref, f32[16,1024]{1,0:T(8,128)S(1)} %get-tuple-element.16.wind_ref, f32[8,1024]{1,0:T(8,128)S(1)} %get-tuple-element.17.trig_ref, ...), custom_call_target="tpu_custom_call" | custom-call | tf_op jit(solution)/shard_map/smooth/pallas_call | solution.py:462
Async XLA Ops:
  0.6 38.1 %copy-start.1 = (f32[1,1,1024]{2,1,0:T(1,128)S(1)}, f32[1,1,1024]{2,1,0:T(1,128)}, u32[]{:S(2)}) copy-start(f32[1,1,1024]{2,1,0:T(1,128)} %param.9) | copy-start | bytes 12292
  2.1 16.2 %all-to-all-start = ((s32[16,1,128]{2,1,0:T(1,128)}), s32[16,1,128]{2,1,0:T(1,128)S(1)}, u32[]{:S(2)}, u32[]{:S(2)}) async-start(s32[16,1,128]{2,1,0:T(1,128)} %ask.1), calls=%async_computation | async-start | bytes 16384 | tf_op jit(solution)/shard_map/all_to_all | solution.py:402
  12.0 0.9 %copy-start = (bf16[48,2048]{1,0:T(8,128)(2,1)S(1)}, bf16[48,2048]{1,0:T(8,128)(2,1)}, u32[]{:S(2)}) copy-start(bf16[48,2048]{1,0:T(8,128)(2,1)} %held_ref.1) | copy-start | bytes 589828
  13.0 0.7 copy-start.2
  20.1 18.6 %all-to-all-start.1 = ((bf16[16,48,512]{2,1,0:T(8,128)(2,1)}), bf16[16,48,512]{2,1,0:T(8,128)(2,1)S(1)}, u32[]{:S(2)}, u32[]{:S(2)}) async-start(bf16[16,48,512]{2,1,0:T(8,128)(2,1)} %select.1), calls=%async_computation.1 | async-start | bytes 1572864 | tf_op jit(solution)/shard_map/all_to_all | solution.py:423

commit v2 on v1

--- a/solution.py
+++ b/solution.py
@@ -21,7 +21,8 @@
 LANES = 128
 MIB = 1 << 20
 HEAD = 1024
-CHUNK = 512
+CHUNK = 256
+PARTS = 4
 F32 = jnp.float32
 BF16 = jnp.bfloat16
 
@@ -69,10 +70,14 @@
     )
 
 
-def ask_kernel(margins_ref, out_ref, margins, sem):
-    copy = pltpu.make_async_copy(margins_ref, margins, sem)
-    copy.start()
-    copy.wait()
+def ask_kernel(margins_ref, checkpoint_ref, asked_ref, held_ref, margins, sems):
+    copies = [
+        pltpu.make_async_copy(margins_ref, margins, sems.at[0]),
+        pltpu.make_async_copy(checkpoint_ref, held_ref, sems.at[1]),
+    ]
+    for copy in copies:
+        copy.start()
+    copies[0].wait()
     reader, lane = iota((N_TILE, LANES), 0), iota((N_TILE, LANES), 1)
     asked = jnp.zeros((N_TILE, LANES), jnp.int32)
     for m in range(GROUPS):
@@ -80,15 +85,28 @@
         asked = jnp.where(reader == (first >> 3), jnp.where(lane == 0, first, second), asked)
     asked = asked & (BLK_DEV - 1)
     for r in range(N_TILE):
-        out_ref[r] = asked[r : r + 1]
-
-
-def prepare_kernel(
-    margins_ref, seams_ref, held_ref, meta_ref, held_out, sem
-):
-    copy = pltpu.make_async_copy(held_ref, held_out, sem)
+        asked_ref[r] = asked[r : r + 1]
+    copies[1].wait()
+
+
+def select_kernel(asked_ref, held_ref, out_ref, staged, sems):
+    copies = []
+    for part in range(PARTS):
+        span = N_TILE // PARTS
+        for g in range(part * span, (part + 1) * span):
+            for j in range(CAP):
+                block = asked_ref[g, j] & (BLK_DEV - 1)
+                staged[g, :, j * SB : (j + 1) * SB] = held_ref[:, pl.ds(pl.multiple_of(block * SB, SB), SB)]
+        where = pl.ds(part * span, span)
+        copies.append(pltpu.make_async_copy(staged.at[where], out_ref.at[where], sems.at[part]))
+        copies[-1].start()
+    for copy in copies:
+        copy.wait()
+
+
+def fetch_kernel(margins_ref, seams_ref, weights_ref, head_ref, meta_ref, sem):
+    copy = pltpu.make_async_copy(weights_ref.at[pl.ds(0, HEAD)], head_ref, sem)
     copy.start()
-
     level, lane = iota((LEV, LANES), 0), iota((LEV, LANES), 1)
     meta = jnp.zeros((LEV, LANES), jnp.int32)
     for m in range(GROUPS):
@@ -96,39 +114,15 @@
         meta = jnp.where((level == 0) & (lane == m), reader, meta)
     for kind in range(3):
         for e in range(4):
-            meta = jnp.where((level == kind + 1) & (lane == e), seams_ref[kind, e], meta)
+            meta = jnp.where((level == kind + 1) & (lane == e), seams_ref[kind, 0, e], meta)
     meta_ref[...] = meta
-    copy.wait()
-
-
-def select_kernel(asked_ref, held_ref, out_ref, sem):
-    copies = []
-    for g in range(N_TILE):
-        for j in range(CAP):
-            block = asked_ref[g, j] & (BLK_DEV - 1)
-            copies.append(
-                pltpu.make_async_copy(
-                    held_ref.at[:, pl.ds(pl.multiple_of(block * SB, SB), SB)],
-                    out_ref.at[g, :, pl.ds(j * SB, SB)],
-                    sem.at[g, j],
-                )
-            )
-    for copy in copies:
-        copy.start()
-    for copy in copies:
-        copy.wait()
-
-
-def fetch_kernel(weights_ref, asked_ref, head_ref, sem):
-    copy = pltpu.make_async_copy(weights_ref.at[pl.ds(0, HEAD)], head_ref, sem)
-    copy.start()
     copy.wait()
 
 
 def remap_kernel(
     meta_ref, blocks_ref, head_ref, weights_ref, angle_ref,
     scalars_ref, wind_ref, trig_ref, place_ref, send_ref,
-    chosen, streamed, pick_ref, scalars_out, sems, out_sem,
+    chosen, streamed, pick_ref, sems,
 ):
     spans = [(k, pl.ds(k, CHUNK)) for k in range(HEAD, K * SB, CHUNK)]
     copies = [
@@ -171,9 +165,7 @@
     for copy, (k, _) in zip(copies, spans):
         copy.wait()
         total = total + dot(chosen[:, k : k + CHUNK], streamed[k - HEAD : k - HEAD + CHUNK])
-    scalars_out[...] = total[WINDS:].astype(BF16)
-    out_copy = pltpu.make_async_copy(scalars_out, scalars_ref, out_sem)
-    out_copy.start()
+    scalars_ref[...] = total[WINDS:].astype(BF16)
     wind = total[:WINDS]
     wind_ref[...] = wind
     east, north = wind[:LEV], wind[LEV:]
@@ -219,11 +211,10 @@
             jnp.where(group == 1, roll(rim[40:48], 32), jnp.where(group == 2, roll(rim[16:24], 32), common_low)),
         )
         send_ref[jnp.clip(meta_ref[1, e], 0, TILES - 1)] = jnp.concatenate([top, low], axis=0).astype(BF16)
-    out_copy.wait()
 
 
 def smooth_kernel(
-    meta_ref, packets_ref, wind_ref, trig_ref, place_ref, dgrid_ref, vortex_ref,
+    meta_ref, packets_ref, wind_ref, trig_ref, place_ref, scalars_ref, scalars_out_ref, dgrid_ref, vortex_ref
 ):
     def packet(tile):
         both = packets_ref[tile].astype(F32)
@@ -232,13 +223,17 @@
     def corner_of(edge, end):
         return jnp.where((edge & 1) == 0, jnp.where(edge == 0, 2, 0) + end, 2 * end + jnp.where(edge == 1, 1, 0))
 
+    scalars_out_ref[...] = scalars_ref[...]
     lane = iota((LEV, LANES), 1)
-    level = iota((LEV, LANES), 0)
     group = lane >> 5
     at = lane & 31
     zero = jnp.zeros((LEV, LANES), F32)
     edges = [meta_ref[2, e] for e in range(4)]
     near = [packet(jnp.clip(meta_ref[1, e], 0, TILES - 1)) for e in range(4)]
+
+    def code_of(top, edge):
+        codes = pltpu.roll(top * 8.0 + roll(top, -4), (LANES - 96 - edge) & 127, 1)
+        return codes[4, 0].astype(jnp.int32)
 
     def strip(half, source):
         out = roll(near[0][half], -32 * source)
@@ -253,56 +248,53 @@
     lane1 = iota((1, LANES), 1)
     edge_of = lane_pick(lane1 >> 5, edges)
 
+    spots = [(e, end) for e in range(4) for end in range(2)]
+
+    def take(into, vector, source, spot):
+        goal = 32 * spot[0] + 31 * spot[1]
+        return jnp.where(lane == goal, pltpu.roll(vector, (goal + LANES - source) & 127, 1), into)
+
+    def mark(into, value, spot):
+        return jnp.where(lane1 == 32 * spot[0] + 31 * spot[1], value, into)
+
+    own_qe, own_qn = zero, zero
+    side_v = jnp.zeros((1, LANES), jnp.int32)
+    sides = []
+    for spot in spots:
+        e, end = spot
+        even = (edges[e] & 1) == 0
+        side = jnp.where(even, 1 if end else 3, 0 if end else 2)
+        corner = corner_of(edges[e], end)
+        beside = jnp.where(even, 2, 1)
+        own_qe = take(own_qe, near[e][1], 96 + 4 * corner + beside, spot)
+        own_qn = take(own_qn, near[e][1], 112 + 4 * corner + beside, spot)
+        side_v = mark(side_v, side, spot)
+        sides.append(side)
+
+    far = []
+    for spot, side in zip(spots, sides):
+        code = code_of(near[spot[0]][0], side)
+        end = (edges[spot[0]] < 2).astype(jnp.int32) ^ (code & 1)
+        far.append((packet(jnp.clip(code >> 3, 0, TILES - 1)), (code >> 1) & 3, end))
+
     far_e, far_n, far_qe, far_qn, far_c, far_cos, far_sin = (zero,) * 7
-    own_qe, own_qn, last_e, last_n = (zero,) * 4
-    side_v = jnp.zeros((1, LANES), jnp.int32)
-    far_edge_v, far_side_v = side_v, side_v
-
-    def code_at(top, e):
-        codes = top * 8.0 + roll(top, -4)
-        return jnp.sum(jnp.where((level == 4) & (lane == 96 + e), codes, 0.0)).astype(jnp.int32)
-
-    for e in range(4):
-        for end in range(2):
-            here = lane == 32 * e + 31 * end
-            here1 = lane1 == 32 * e + 31 * end
-            goal = 32 * e + 31 * end + LANES
-
-            def take(into, vector, source):
-                return jnp.where(here, pltpu.roll(vector, (goal - source) & 127, 1), into)
-
-            even = (edges[e] & 1) == 0
-            side = jnp.where(even, 1 if end else 3, 0 if end else 2)
-            high = (edges[e] < 2).astype(jnp.int32)
-            c2 = corner_of(edges[e], end)
-            q2 = jnp.where(even, 2, 1)
-            own_qe = take(own_qe, near[e][1], 96 + 4 * c2 + q2)
-            own_qn = take(own_qn, near[e][1], 112 + 4 * c2 + q2)
-            code = code_at(near[e][0], side)
-            far_edge, far_flip = (code >> 1) & 3, code & 1
-            far_top, far_low = packet(jnp.clip(code >> 3, 0, TILES - 1))
-            end3 = high ^ far_flip
-            c3 = corner_of(far_edge, end3)
-            q3 = jnp.where((far_edge & 1) == 0, 1, 2)
-            far_e = take(far_e, far_low, 96 + 4 * c3)
-            far_n = take(far_n, far_low, 112 + 4 * c3)
-            far_qe = take(far_qe, far_low, 96 + 4 * c3 + q3)
-            far_qn = take(far_qn, far_low, 112 + 4 * c3 + q3)
-            far_c = take(far_c, far_low, 96 + 4 * c3 + 3)
-            far_trig = take(zero, far_top, 96 + 4 * c3)
-            far_cos, far_sin = far_cos + far_trig[6:7], far_sin + far_trig[5:6]
-            far_side = jnp.where(
-                (far_edge & 1) == 0, jnp.where(end3 == 1, 1, 3), jnp.where(end3 == 1, 0, 2)
-            )
-            code = code_at(far_top, far_side)
-            last_edge, last_flip = (code >> 1) & 3, code & 1
-            _, last_low = packet(jnp.clip(code >> 3, 0, TILES - 1))
-            c4 = corner_of(last_edge, (far_edge < 2).astype(jnp.int32) ^ last_flip)
-            last_e = take(last_e, last_low, 96 + 4 * c4)
-            last_n = take(last_n, last_low, 112 + 4 * c4)
-            side_v = jnp.where(here1, side, side_v)
-            far_edge_v = jnp.where(here1, far_edge, far_edge_v)
-            far_side_v = jnp.where(here1, far_side, far_side_v)
+    far_edge_v, far_side_v = jnp.zeros_like(side_v), jnp.zeros_like(side_v)
+    sides = []
+    for spot, ((top, low), edge, end) in zip(spots, far):
+        corner = corner_of(edge, end)
+        even = (edge & 1) == 0
+        beside = jnp.where(even, 1, 2)
+        side = jnp.where(even, jnp.where(end == 1, 1, 3), jnp.where(end == 1, 0, 2))
+        far_e = take(far_e, low, 96 + 4 * corner, spot)
+        far_n = take(far_n, low, 112 + 4 * corner, spot)
+        far_qe = take(far_qe, low, 96 + 4 * corner + beside, spot)
+        far_qn = take(far_qn, low, 112 + 4 * corner + beside, spot)
+        far_c = take(far_c, low, 96 + 4 * corner + 3, spot)
+        trig = take(zero, top, 96 + 4 * corner, spot)
+        far_cos, far_sin = far_cos + trig[6:7], far_sin + trig[5:6]
+        far_edge_v = mark(far_edge_v, edge, spot)
+        far_side_v = mark(far_side_v, side, spot)
+        sides.append(side)
 
     place = place_ref[...]
     cell = iota((1, CELLS), 1)
@@ -336,26 +328,36 @@
     cosine, sine = trig_ref[0:1, :], trig_ref[1:2, :]
     rim = rims_of(wind)
     rim_e, rim_n = rim[:LEV], rim[LEV:]
-    halo_e, halo_n = placed([(east_hi, east_lo), (north_hi, north_lo)])
+
+    c0 = c0 + towards(edge_of, cos0, sin0, rim_e - east0, rim_n - north0)
+    ends = (at == 0) | (at == 31)
+    c0 = c0 + jnp.where(ends, towards(side_v, cos0, sin0, far_e - east0, far_n - north0), 0.0)
+    c1 = c1 + jnp.where(ends, towards(side_v, cos1, sin1, far_qe - own_qe, far_qn - own_qn), 0.0)
+    far_c = far_c + towards(far_edge_v, far_cos, far_sin, east0 - far_e, north0 - far_n)
+
+    last_e, last_n = zero, zero
+    for index, (spot, side) in enumerate(zip(spots, sides)):
+        code = code_of(far[index][0][0], side)
+        end = (far[index][1] < 2).astype(jnp.int32) ^ (code & 1)
+        corner = corner_of((code >> 1) & 3, end)
+        _, low = packet(jnp.clip(code >> 3, 0, TILES - 1))
+        last_e = take(last_e, low, 96 + 4 * corner, spot)
+        last_n = take(last_n, low, 112 + 4 * corner, spot)
+    far_c = far_c + towards(far_side_v, far_cos, far_sin, last_e - far_e, last_n - far_n)
+    after = jnp.where(at == 31, far_c, roll(c0, -1))
+    before = jnp.where(at == 0, far_c, roll(c0, 1))
+    s0 = c0 + 0.2 * (c1 + after + before - 4.0 * c0)
+    halo_e, halo_n, halo_c, halo_s = placed(
+        [(east_hi, east_lo), (north_hi, north_lo), halves(c0), halves(s0)]
+    )
+
     ex, exm, ey, eym = shifts(east, halo_e)
     nx, nxm, ny, nym = shifts(north, halo_n)
     along = cosine * (0.5 * (east + ey)) + sine * (0.5 * (north + ny))
     across = -sine * (0.5 * (east + ex)) + cosine * (0.5 * (north + nx))
     dgrid_ref[...] = jnp.concatenate([along, across], axis=0).astype(BF16)
     vortex = cosine * (0.5 * (nx - nxm) - 0.5 * (ey - eym)) - sine * (0.5 * (ex - exm) + 0.5 * (ny - nym))
-
-    c0 = c0 + towards(edge_of, cos0, sin0, rim_e - east0, rim_n - north0)
-    ends = (at == 0) | (at == 31)
-    c0 = c0 + jnp.where(ends, towards(side_v, cos0, sin0, far_e - east0, far_n - north0), 0.0)
-    c1 = c1 + jnp.where(ends, towards(side_v, cos1, sin1, far_qe - own_qe, far_qn - own_qn), 0.0)
-    far_c = far_c + towards(far_edge_v, far_cos, far_sin, east0 - far_e, north0 - far_n)
-    far_c = far_c + towards(far_side_v, far_cos, far_sin, last_e - far_e, last_n - far_n)
-
-    rim_c = rims_of(vortex)
-    after = jnp.where(at == 31, far_c, roll(c0, -1))
-    before = jnp.where(at == 0, far_c, roll(c0, 1))
-    s0 = c0 + 0.2 * (c1 + rim_c + after + before - 4.0 * c0)
-    halo_c, halo_s = placed([halves(c0), halves(s0)])
+    halo_s = tuple(h + 0.2 * vortex for h in halo_s)
     for halo in (halo_c, halo_s):
         xp, xm, yp, ym = shifts(vortex, halo)
         vortex = vortex + 0.2 * (xp + xm + yp + ym - 4.0 * vortex)
@@ -391,48 +393,45 @@
     weights = remap_weights[0, 0].reshape(K * SB, CELLS)
     limit = pltpu.CompilerParams(vmem_limit_bytes=16 * MIB)
 
-    asked = pl.pallas_call(
+    def in_hbm(x):
+        return pltpu.with_memory_space_constraint(x, pltpu.HBM)
+
+    asked, held = pl.pallas_call(
         ask_kernel,
-        out_shape=shape((N_TILE, 1, LANES), jnp.int32),
-        in_specs=[hbm()],
-        out_specs=vmem(),
-        scratch_shapes=[pltpu.SMEM((K,), jnp.int32), pltpu.SemaphoreType.DMA],
+        out_shape=(shape((N_TILE, 1, LANES), jnp.int32), shape(checkpoint.shape, BF16)),
+        in_specs=[hbm(), hbm()],
+        out_specs=(vmem(),) * 2,
+        scratch_shapes=[pltpu.SMEM((K,), jnp.int32), pltpu.SemaphoreType.DMA((2,))],
+        compiler_params=limit,
         name="ask",
-    )(own_margins)
+    )(in_hbm(own_margins), in_hbm(checkpoint))
     asked = lax.all_to_all(asked, "tile", 0, 0, tiled=True).reshape(N_TILE, LANES)
-
-    meta, held = pl.pallas_call(
-        prepare_kernel,
-        out_shape=(shape((LEV, LANES), jnp.int32), shape(checkpoint.shape, BF16)),
-        in_specs=[smem(), smem(), hbm()],
-        out_specs=(vmem(),) * 2,
-        scratch_shapes=[pltpu.SemaphoreType.DMA],
-        compiler_params=limit,
-        cost_estimate=cost(1 << 20, MIB),
-        name="prepare",
-    )(own_margins, seams[0, 0], checkpoint)
+    asked, own_margins, own_seams, angle = lax.optimization_barrier(
+        (asked, own_margins, seams.reshape(3, 1, 4), rotation_angle[0, 0].reshape(1, CELLS))
+    )
+
     blocks = pl.pallas_call(
         select_kernel,
         out_shape=shape((N_TILE, ROWS, CAP * SB), BF16),
         in_specs=[smem(), vmem()],
         out_specs=anywhere(),
-        scratch_shapes=[pltpu.SemaphoreType.DMA((N_TILE, CAP))],
+        scratch_shapes=[pltpu.VMEM((N_TILE, ROWS, CAP * SB), BF16), pltpu.SemaphoreType.DMA((PARTS,))],
         compiler_params=limit,
         name="select",
     )(asked, held)
     blocks = lax.all_to_all(blocks, "tile", 0, 0, tiled=True)
 
-    weights = pltpu.with_memory_space_constraint(weights, pltpu.HBM)
-    head = pl.pallas_call(
+    weights = in_hbm(weights)
+    head, meta = pl.pallas_call(
         fetch_kernel,
-        out_shape=shape((HEAD, CELLS), BF16),
-        in_specs=[hbm(), anywhere()],
-        out_specs=vmem(),
+        out_shape=(shape((HEAD, CELLS), BF16), shape((LEV, LANES), jnp.int32)),
+        in_specs=[smem(), smem(), hbm()],
+        out_specs=(vmem(),) * 2,
         scratch_shapes=[pltpu.SemaphoreType.DMA],
         compiler_params=limit,
         cost_estimate=cost(1 << 20, 4 * MIB),
         name="fetch",
-    )(weights, asked)
+    )(own_margins, own_seams, weights)
 
     scalars, wind, trig, place, packets = pl.pallas_call(
         remap_kernel,
@@ -444,29 +443,31 @@
             shape((TILES, 16, LANES), BF16),
         ),
         in_specs=[smem(), vmem(), vmem(), hbm(), vmem()],
-        out_specs=(anywhere(),) + (vmem(),) * 4,
+        out_specs=(vmem(),) * 5,
         scratch_shapes=[
             pltpu.VMEM((ROWS, K * SB), BF16),
             pltpu.VMEM((K * SB - HEAD, CELLS), BF16),
             pltpu.VMEM((CELLS, 3 * LANES), BF16),
-            pltpu.VMEM((ROWS - WINDS, CELLS), BF16),
             pltpu.SemaphoreType.DMA(((K * SB - HEAD) // CHUNK,)),
-            pltpu.SemaphoreType.DMA,
         ],
         compiler_params=limit,
         cost_estimate=cost(2 * ROWS * K * SB * CELLS, 9 * MIB),
         name="remap",
-    )(meta, blocks, head, weights, rotation_angle[0, 0].reshape(1, CELLS))
+    )(meta, blocks, head, weights, angle)
     packets = lax.all_to_all(packets, ("face", "tile"), 0, 0, tiled=True)
 
-    dgrid, vortex = pl.pallas_call(
+    scalars, dgrid, vortex = pl.pallas_call(
         smooth_kernel,
-        out_shape=(shape((WINDS, CELLS), BF16), shape((LEV, CELLS), F32)),
-        in_specs=[smem()] + [vmem()] * 4,
-        out_specs=(vmem(), vmem()),
+        out_shape=(
+            shape((ROWS - WINDS, CELLS), BF16),
+            shape((WINDS, CELLS), BF16),
+            shape((LEV, CELLS), F32),
+        ),
+        in_specs=[smem()] + [vmem()] * 5,
+        out_specs=(vmem(),) * 3,
         compiler_params=limit,
         name="smooth",
-    )(meta, packets, wind, trig, place)
+    )(meta, packets, wind, trig, place, scalars)
     return (
         scalars.reshape(1, 1, ROWS - WINDS, CELLS),
         dgrid.reshape(1, 1, WINDS, CELLS),

time: 66.4 us -> 63.9 us (0.962)
  blocking collectives: 19.4 us -> 35.5 us
  starting transfers between devices: 13.4 us -> 4.08 us
  waiting for transfers between devices: 16.7 us -> 11 us
  Pallas kernels: 13.6 us -> 11 us
  local copies, waits for them, and re-layouts: 2.27 us -> 1.33 us
    all_to_all x0 -> x1, blocking collectives: none -> 16.1 us  [body(): lax.all_to_all(asked, 'tile', 0, 0, tiled=True).reshape(N_TILE, LANES)]
    all_to_all x1 -> x0, starting transfers between devices: 9.3 us -> none  [body(): lax.all_to_all(asked, 'tile', 0, 0, tiled=True).reshape(N_TILE, LANES)]
    all_to_all x1 -> x0, waiting for transfers between devices: 3.78 us -> none  [body(): lax.all_to_all(asked, 'tile', 0, 0, tiled=True).reshape(N_TILE, LANES)]
    pallas_call x4 -> x3, Pallas kernels: 7.2 us -> 5.27 us  [the longest x1 2.16 us: body(): pl.pallas_call(smooth_kernel, out_shape=(shape((ROWS - WINDS, CELLS), BF1...]
    all_to_all x1, waiting for transfers between devices: 12.9 us -> 11 us  [body(): blocks = lax.all_to_all(blocks, 'tile', 0, 0, tiled=True)]
    unnamed x7 -> x6, local copies, waits for them, and re-layouts: 2.27 us -> 1.33 us
  transfers between devices with their start and end apart: 2 -> 1, of which waited for: 2 -> 1; matrix products, arithmetic and copies ran while one was open for 1% -> 0% of each run, Pallas kernels for 4% -> 3%
where the time goes in v2:
time: 63.9 us; the launch traced here: 63.6 us
  blocking collectives  35.5 us (56%)
  Pallas kernels  11 us (17%)
  waiting for transfers between devices  11 us (17%)
  starting transfers between devices  4.08 us (6%)
  local copies, waits for them, and re-layouts  1.33 us (2%)
  between operations  0.68 us (1%)
    all_to_all x1, blocking collectives, body(): packets = lax.all_to_all(packets, ('face', 'tile'), 0, 0, tiled=True)  19.4 us
    all_to_all x1, blocking collectives, body(): lax.all_to_all(asked, 'tile', 0, 0, tiled=True).reshape(N_TILE, LANES)  16.1 us
    all_to_all x1, waiting for transfers between devices, body(): blocks = lax.all_to_all(blocks, 'tile', 0, 0, tiled=True)  11 us
    pallas_call x1, Pallas kernels, body(): pl.pallas_call(remap_kernel, out_shape=(shape((ROWS - WINDS, CELLS), BF16...  4.14 us
    all_to_all x1, starting transfers between devices, body(): blocks = lax.all_to_all(blocks, 'tile', 0, 0, tiled=True)  4.08 us
    pallas_call x1, Pallas kernels, body(): pl.pallas_call(smooth_kernel, out_shape=(shape((ROWS - WINDS, CELLS), BF1...  2.16 us
    pallas_call x1, Pallas kernels, body(): pl.pallas_call(fetch_kernel, out_shape=(shape((HEAD, CELLS), BF16), shape...  2.16 us
    pallas_call x1, Pallas kernels, body(): pl.pallas_call(select_kernel, out_shape=shape((N_TILE, ROWS, CAP * SB), B...  1.62 us
  transfers between devices with their start and end apart: 1, of which 1 were waited for; matrix products, arithmetic and copies ran while one was open for 0% of the time, Pallas kernels for 3%

profile of v2, /device:TPU:1, one launch (start us, length us, event | category | flops | bytes accessed | tf_op | source)
XLA Modules:
  0.0 63.6 jit_solution(3954219841497770243)
XLA Ops:
  0.6 0.0 copy-start
  0.6 1.0 %ask.1 = (s32[16,1,128]{2,1,0:T(1,128)S(1)}, bf16[48,2048]{1,0:T(8,128)(2,1)S(1)}) custom-call(s32[16]{0:T(128)} %bitcast.10, bf16[48,2048]{1,0:T(8,128)(2,1)} %checkpoint_ref.1), custom_call_target="tpu_custom_call" | custom-call | tf_op jit(solution)/shard_map/ask/pallas_call | solution.py:399
  1.6 16.1 %all_to_all.15 = s32[16,1,128]{2,1,0:T(1,128)S(1)} all-to-all(s32[16,1,128]{2,1,0:T(1,128)S(1)} %get-tuple-element.19), channel_id=1, replica_groups=mesh['face'=8,'tile'=16] {'tile'}, dimensions={0} | all-to-all | bytes 16384 | tf_op jit(solution)/shard_map/all_to_all | solution.py:408
  17.7 1.6 %select.1 = bf16[16,48,512]{2,1,0:T(8,128)(2,1)} custom-call(s32[16,128]{1,0:T(8,128)S(1)} %bitcast.8, bf16[48,2048]{1,0:T(8,128)(2,1)S(1)} %get-tuple-element.24.held_ref), custom_call_target="tpu_custom_call" | custom-call | tf_op jit(solution)/shard_map/select/pallas_call | solution.py:413
  19.3 4.1 %all-to-all-start.1 = ((bf16[16,48,512]{2,1,0:T(8,128)(2,1)}), bf16[16,48,512]{2,1,0:T(8,128)(2,1)S(1)}, u32[]{:S(2)}, u32[]{:S(2)}) async-start(bf16[16,48,512]{2,1,0:T(8,128)(2,1)} %select.1), calls=%async_computation.1 | async-start | bytes 1572864 | tf_op jit(solution)/shard_map/all_to_all | solution.py:422
  23.4 0.0 copy-start.1
  23.4 0.6 %copy-done.1 = s32[1,1,16]{2,1,0:T(1,128)S(1)} copy-done((s32[1,1,16]{2,1,0:T(1,128)S(1)}, s32[1,1,16]{2,1,0:T(1,128)}, u32[]{:S(2)}) %copy-start.1) | copy-done | bytes 88
  24.0 0.0 copy-start.2
  24.0 0.7 %copy-done.2 = s32[1,1,3,4]{3,1,2,0:T(1,128)S(1)} copy-done((s32[1,1,3,4]{3,1,2,0:T(1,128)S(1)}, s32[1,1,3,4]{3,1,2,0:T(1,128)}, u32[]{:S(2)}) %copy-start.2) | copy-done | bytes 72
  24.7 2.2 %fetch.1 = (bf16[1024,1024]{1,0:T(8,128)(2,1)S(1)}, s32[8,128]{1,0:T(8,128)S(1)}) custom-call(s32[16]{0:T(128)S(1)} %bitcast.11, s32[3,1,4]{2,1,0:T(1,128)S(1)} %bitcast.12, bf16[4096,1024]{1,0:T(8,128)(2,1)} %bitcast.13), custom_call_target="tpu_custom_call" | custom-call | flops 1048576 | bytes 4194304 | tf_op jit(solution)/shard_map/fetch/pallas_call | solution.py:425
  26.9 11.0 %all-to-all-done.1.blocks_ref = bf16[16,48,512]{2,1,0:T(8,128)(2,1)S(1)} async-done(((bf16[16,48,512]{2,1,0:T(8,128)(2,1)}), bf16[16,48,512]{2,1,0:T(8,128)(2,1)S(1)}, u32[]{:S(2)}, u32[]{:S(2)}) %all-to-all-start.1) | async-done | bytes 786464 | tf_op jit(solution)/shard_map/all_to_all | solution.py:422
  37.9 0.0 copy-done
  37.9 4.1 %remap.1 = (bf16[32,1024]{1,0:T(8,128)(2,1)S(1)}, f32[16,1024]{1,0:T(8,128)S(1)}, f32[8,1024]{1,0:T(8,128)S(1)}, bf16[128,1024]{1,0:T(8,128)(2,1)S(1)}, bf16[128,16,128]{2,1,0:T(8,128)(2,1)S(1)}) custom-call(s32[8,128]{1,0:T(8,128)S(1)} %get-tuple-element.22.meta_ref, bf16[16,48,512]{2,1,0:T(8,128)(2,1)S(1)} %all-to-all-done.1.blocks_ref, ...), custom_call_target="tpu_custom_call" | custom-call | flops 402653184 | bytes 9437184 | tf_op jit(solution)/shard_map/remap/pallas_call | solution.py:436
  42.0 19.4 %all_to_all.16.packets_ref = bf16[128,16,128]{2,1,0:T(8,128)(2,1)S(1)} all-to-all(bf16[128,16,128]{2,1,0:T(8,128)(2,1)S(1)} %get-tuple-element.27), channel_id=1, replica_groups=mesh['face'=8,'tile'=16] {'face','tile'}, dimensions={0} | all-to-all | bytes 1048576 | tf_op jit(solution)/shard_map/all_to_all | solution.py:457
  61.4 2.2 %smooth.1 = (bf16[32,1024]{1,0:T(8,128)(2,1)}, bf16[16,1024]{1,0:T(8,128)(2,1)}, f32[8,1024]{1,0:T(8,128)}) custom-call(s32[8,128]{1,0:T(8,128)S(1)} %get-tuple-element.22.meta_ref, bf16[128,16,128]{2,1,0:T(8,128)(2,1)S(1)} %all_to_all.16.packets_ref, f32[16,1024]{1,0:T(8,128)S(1)} %get-tuple-element.28.wind_ref, f32[8,1024]{1,0:T(8,128)S(1)} %get-tuple-element.29.trig_ref, ...), custom_call_target="tpu_custom_call" | custom-call | tf_op jit(solution)/shard_map/smooth/pallas_call | solution.py:459
Async XLA Ops:
  0.6 37.2 %copy-start = (f32[1,1,1024]{2,1,0:T(1,128)S(1)}, f32[1,1,1024]{2,1,0:T(1,128)}, u32[]{:S(2)}) copy-start(f32[1,1,1024]{2,1,0:T(1,128)} %param.9) | copy-start | bytes 12292
  19.3 18.6 %all-to-all-start.1 = ((bf16[16,48,512]{2,1,0:T(8,128)(2,1)}), bf16[16,48,512]{2,1,0:T(8,128)(2,1)S(1)}, u32[]{:S(2)}, u32[]{:S(2)}) async-start(bf16[16,48,512]{2,1,0:T(8,128)(2,1)} %select.1), calls=%async_computation.1 | async-start | bytes 1572864 | tf_op jit(solution)/shard_map/all_to_all | solution.py:422
  23.4 0.7 %copy-start.1 = (s32[1,1,16]{2,1,0:T(1,128)S(1)}, s32[1,1,16]{2,1,0:T(1,128)}, u32[]{:S(2)}) copy-start(s32[1,1,16]{2,1,0:T(1,128)} %param.7) | copy-start | bytes 196
  24.0 0.7 %copy-start.2 = (s32[1,1,3,4]{3,1,2,0:T(1,128)S(1)}, s32[1,1,3,4]{3,1,2,0:T(1,128)}, u32[]{:S(2)}) copy-start(s32[1,1,3,4]{3,1,2,0:T(1,128)} %param.8) | copy-start | bytes 148

commit v3 on v2

--- a/solution.py
+++ b/solution.py
@@ -20,9 +20,7 @@
 WINDS = 2 * LEV
 LANES = 128
 MIB = 1 << 20
-HEAD = 1024
 CHUNK = 256
-PARTS = 4
 F32 = jnp.float32
 BF16 = jnp.bfloat16
 
@@ -70,10 +68,13 @@
     )
 
 
-def ask_kernel(margins_ref, checkpoint_ref, asked_ref, held_ref, margins, sems):
+def ask_kernel(
+    margins_ref, seams_ref, checkpoint_ref, asked_ref, meta_ref, held_ref, margins, seams, sems
+):
     copies = [
         pltpu.make_async_copy(margins_ref, margins, sems.at[0]),
-        pltpu.make_async_copy(checkpoint_ref, held_ref, sems.at[1]),
+        pltpu.make_async_copy(seams_ref, seams, sems.at[1]),
+        pltpu.make_async_copy(checkpoint_ref, held_ref, sems.at[2]),
     ]
     for copy in copies:
         copy.start()
@@ -86,57 +87,52 @@
     asked = asked & (BLK_DEV - 1)
     for r in range(N_TILE):
         asked_ref[r] = asked[r : r + 1]
+
     copies[1].wait()
-
-
-def select_kernel(asked_ref, held_ref, out_ref, staged, sems):
-    copies = []
-    for part in range(PARTS):
-        span = N_TILE // PARTS
-        for g in range(part * span, (part + 1) * span):
-            for j in range(CAP):
-                block = asked_ref[g, j] & (BLK_DEV - 1)
-                staged[g, :, j * SB : (j + 1) * SB] = held_ref[:, pl.ds(pl.multiple_of(block * SB, SB), SB)]
-        where = pl.ds(part * span, span)
-        copies.append(pltpu.make_async_copy(staged.at[where], out_ref.at[where], sems.at[part]))
-        copies[-1].start()
-    for copy in copies:
-        copy.wait()
-
-
-def fetch_kernel(margins_ref, seams_ref, weights_ref, head_ref, meta_ref, sem):
-    copy = pltpu.make_async_copy(weights_ref.at[pl.ds(0, HEAD)], head_ref, sem)
-    copy.start()
     level, lane = iota((LEV, LANES), 0), iota((LEV, LANES), 1)
     meta = jnp.zeros((LEV, LANES), jnp.int32)
     for m in range(GROUPS):
-        reader = jnp.clip(margins_ref[CAP * m] >> 3, 0, N_TILE - 1)
+        reader = jnp.clip(margins[CAP * m] >> 3, 0, N_TILE - 1)
         meta = jnp.where((level == 0) & (lane == m), reader, meta)
     for kind in range(3):
         for e in range(4):
-            meta = jnp.where((level == kind + 1) & (lane == e), seams_ref[kind, 0, e], meta)
+            meta = jnp.where((level == kind + 1) & (lane == e), seams[kind, 0, e], meta)
     meta_ref[...] = meta
-    copy.wait()
+    copies[2].wait()
+
+
+def slot(tile):
+    tile = jnp.clip(tile, 0, TILES - 1)
+    return (tile & (N_TILE - 1)) * (TILES // N_TILE) + (tile >> 4)
+
+
+def select_kernel(asked_ref, held_ref, out_ref):
+    for g in range(N_TILE):
+        for j in range(CAP):
+            block = asked_ref[g, j] & (BLK_DEV - 1)
+            out_ref[g, :, j * SB : (j + 1) * SB] = held_ref[:, pl.ds(pl.multiple_of(block * SB, SB), SB)]
 
 
 def remap_kernel(
-    meta_ref, blocks_ref, head_ref, weights_ref, angle_ref,
+    meta_ref, blocks_ref, weights_ref, angle_ref,
     scalars_ref, wind_ref, trig_ref, place_ref, send_ref,
-    chosen, streamed, pick_ref, sems,
+    chosen, streamed, pick_ref, angle, sems,
 ):
-    spans = [(k, pl.ds(k, CHUNK)) for k in range(HEAD, K * SB, CHUNK)]
+    angle_copy = pltpu.make_async_copy(angle_ref, angle, sems.at[K * SB // CHUNK])
+    angle_copy.start()
+    spans = [(k, pl.ds(k, CHUNK)) for k in range(0, K * SB, CHUNK)]
     copies = [
-        pltpu.make_async_copy(weights_ref.at[span], streamed.at[pl.ds(k - HEAD, CHUNK)], sems.at[index])
+        pltpu.make_async_copy(weights_ref.at[span], streamed.at[span], sems.at[index])
         for index, (k, span) in enumerate(spans)
     ]
     for copy in copies:
         copy.start()
     for m in range(GROUPS):
         chosen[:, CAP * SB * m : CAP * SB * (m + 1)] = blocks_ref[meta_ref[0, m]]
-    total = dot(chosen[:, :HEAD], head_ref[...])
-
-    angle = angle_ref[...]
-    trig_ref[...] = jnp.where((iota((LEV, CELLS), 0) & 1) == 0, jnp.cos(angle), jnp.sin(angle))
+    total = None
+
+    angle_copy.wait()
+    trig_ref[...] = jnp.where((iota((LEV, CELLS), 0) & 1) == 0, jnp.cos(angle[...]), jnp.sin(angle[...]))
 
     lane = iota((1, 3 * LANES), 1)
     edge, depth, at = (lane >> 6) & 3, (lane >> 5) & 1, lane & 31
@@ -164,7 +160,8 @@
 
     for copy, (k, _) in zip(copies, spans):
         copy.wait()
-        total = total + dot(chosen[:, k : k + CHUNK], streamed[k - HEAD : k - HEAD + CHUNK])
+        part = dot(chosen[:, k : k + CHUNK], streamed[k : k + CHUNK])
+        total = part if total is None else total + part
     scalars_ref[...] = total[WINDS:].astype(BF16)
     wind = total[:WINDS]
     wind_ref[...] = wind
@@ -210,14 +207,14 @@
             group == 0, rim[8:16],
             jnp.where(group == 1, roll(rim[40:48], 32), jnp.where(group == 2, roll(rim[16:24], 32), common_low)),
         )
-        send_ref[jnp.clip(meta_ref[1, e], 0, TILES - 1)] = jnp.concatenate([top, low], axis=0).astype(BF16)
+        send_ref[slot(meta_ref[1, e])] = jnp.concatenate([top, low], axis=0).astype(BF16)
 
 
 def smooth_kernel(
     meta_ref, packets_ref, wind_ref, trig_ref, place_ref, scalars_ref, scalars_out_ref, dgrid_ref, vortex_ref
 ):
     def packet(tile):
-        both = packets_ref[tile].astype(F32)
+        both = packets_ref[slot(tile)].astype(F32)
         return both[:LEV], both[LEV:]
 
     def corner_of(edge, end):
@@ -229,7 +226,7 @@
     at = lane & 31
     zero = jnp.zeros((LEV, LANES), F32)
     edges = [meta_ref[2, e] for e in range(4)]
-    near = [packet(jnp.clip(meta_ref[1, e], 0, TILES - 1)) for e in range(4)]
+    near = [packet(meta_ref[1, e]) for e in range(4)]
 
     def code_of(top, edge):
         codes = pltpu.roll(top * 8.0 + roll(top, -4), (LANES - 96 - edge) & 127, 1)
@@ -275,7 +272,7 @@
     for spot, side in zip(spots, sides):
         code = code_of(near[spot[0]][0], side)
         end = (edges[spot[0]] < 2).astype(jnp.int32) ^ (code & 1)
-        far.append((packet(jnp.clip(code >> 3, 0, TILES - 1)), (code >> 1) & 3, end))
+        far.append((packet(code >> 3), (code >> 1) & 3, end))
 
     far_e, far_n, far_qe, far_qn, far_c, far_cos, far_sin = (zero,) * 7
     far_edge_v, far_side_v = jnp.zeros_like(side_v), jnp.zeros_like(side_v)
@@ -340,7 +337,7 @@
         code = code_of(far[index][0][0], side)
         end = (far[index][1] < 2).astype(jnp.int32) ^ (code & 1)
         corner = corner_of((code >> 1) & 3, end)
-        _, low = packet(jnp.clip(code >> 3, 0, TILES - 1))
+        _, low = packet(code >> 3)
         last_e = take(last_e, low, 96 + 4 * corner, spot)
         last_n = take(last_n, low, 112 + 4 * corner, spot)
     far_c = far_c + towards(far_side_v, far_cos, far_sin, last_e - far_e, last_n - far_n)
@@ -389,49 +386,39 @@
 
 
 def body(checkpoint, remap_weights, margins, seams, rotation_angle):
-    own_margins = margins[0, 0]
     weights = remap_weights[0, 0].reshape(K * SB, CELLS)
     limit = pltpu.CompilerParams(vmem_limit_bytes=16 * MIB)
 
     def in_hbm(x):
         return pltpu.with_memory_space_constraint(x, pltpu.HBM)
 
-    asked, held = pl.pallas_call(
+    asked, meta, held = pl.pallas_call(
         ask_kernel,
-        out_shape=(shape((N_TILE, 1, LANES), jnp.int32), shape(checkpoint.shape, BF16)),
-        in_specs=[hbm(), hbm()],
-        out_specs=(vmem(),) * 2,
-        scratch_shapes=[pltpu.SMEM((K,), jnp.int32), pltpu.SemaphoreType.DMA((2,))],
+        out_shape=(
+            shape((N_TILE, 1, LANES), jnp.int32),
+            shape((LEV, LANES), jnp.int32),
+            shape(checkpoint.shape, BF16),
+        ),
+        in_specs=[hbm()] * 3,
+        out_specs=(vmem(),) * 3,
+        scratch_shapes=[
+            pltpu.SMEM((K,), jnp.int32),
+            pltpu.SMEM((3, 1, 4), jnp.int32),
+            pltpu.SemaphoreType.DMA((3,)),
+        ],
         compiler_params=limit,
         name="ask",
-    )(in_hbm(own_margins), in_hbm(checkpoint))
+    )(in_hbm(margins[0, 0]), in_hbm(seams.reshape(3, 1, 4)), in_hbm(checkpoint))
     asked = lax.all_to_all(asked, "tile", 0, 0, tiled=True).reshape(N_TILE, LANES)
-    asked, own_margins, own_seams, angle = lax.optimization_barrier(
-        (asked, own_margins, seams.reshape(3, 1, 4), rotation_angle[0, 0].reshape(1, CELLS))
-    )
-
     blocks = pl.pallas_call(
         select_kernel,
         out_shape=shape((N_TILE, ROWS, CAP * SB), BF16),
         in_specs=[smem(), vmem()],
-        out_specs=anywhere(),
-        scratch_shapes=[pltpu.VMEM((N_TILE, ROWS, CAP * SB), BF16), pltpu.SemaphoreType.DMA((PARTS,))],
+        out_specs=vmem(),
         compiler_params=limit,
         name="select",
     )(asked, held)
     blocks = lax.all_to_all(blocks, "tile", 0, 0, tiled=True)
-
-    weights = in_hbm(weights)
-    head, meta = pl.pallas_call(
-        fetch_kernel,
-        out_shape=(shape((HEAD, CELLS), BF16), shape((LEV, LANES), jnp.int32)),
-        in_specs=[smem(), smem(), hbm()],
-        out_specs=(vmem(),) * 2,
-        scratch_shapes=[pltpu.SemaphoreType.DMA],
-        compiler_params=limit,
-        cost_estimate=cost(1 << 20, 4 * MIB),
-        name="fetch",
-    )(own_margins, own_seams, weights)
 
     scalars, wind, trig, place, packets = pl.pallas_call(
         remap_kernel,
@@ -442,19 +429,20 @@
             shape((LANES, CELLS), BF16),
             shape((TILES, 16, LANES), BF16),
         ),
-        in_specs=[smem(), vmem(), vmem(), hbm(), vmem()],
+        in_specs=[smem(), vmem(), hbm(), hbm()],
         out_specs=(vmem(),) * 5,
         scratch_shapes=[
             pltpu.VMEM((ROWS, K * SB), BF16),
-            pltpu.VMEM((K * SB - HEAD, CELLS), BF16),
+            pltpu.VMEM((K * SB, CELLS), BF16),
             pltpu.VMEM((CELLS, 3 * LANES), BF16),
-            pltpu.SemaphoreType.DMA(((K * SB - HEAD) // CHUNK,)),
+            pltpu.VMEM((1, CELLS), F32),
+            pltpu.SemaphoreType.DMA((K * SB // CHUNK + 1,)),
         ],
         compiler_params=limit,
         cost_estimate=cost(2 * ROWS * K * SB * CELLS, 9 * MIB),
         name="remap",
-    )(meta, blocks, head, weights, angle)
-    packets = lax.all_to_all(packets, ("face", "tile"), 0, 0, tiled=True)
+    )(meta, blocks, in_hbm(weights), in_hbm(rotation_angle[0, 0].reshape(1, CELLS)))
+    packets = lax.all_to_all(packets, ("tile", "face"), 0, 0, tiled=True)
 
     scalars, dgrid, vortex = pl.pallas_call(
         smooth_kernel,

time: 63.9 us -> 62 us (0.970)
  blocking collectives: 35.5 us -> 52.5 us
  waiting for transfers between devices: 11 us -> 0 us
  starting transfers between devices: 4.08 us -> 0 us
  Pallas kernels: 11 us -> 8.7 us
  local copies, waits for them, and re-layouts: 1.33 us -> 0 us
    all_to_all x1 -> x2, blocking collectives: 19.4 us -> 36.4 us  [the longest x1 18.9 us: body(): packets = lax.all_to_all(packets, ('tile', 'face'), 0, 0, tiled=True)]
    all_to_all x1 -> x0, waiting for transfers between devices: 11 us -> none  [body(): blocks = lax.all_to_all(blocks, 'tile', 0, 0, tiled=True)]
    all_to_all x1 -> x0, starting transfers between devices: 4.08 us -> none  [body(): blocks = lax.all_to_all(blocks, 'tile', 0, 0, tiled=True)]
    pallas_call x1 -> x0, Pallas kernels: 2.16 us -> none  [body(): pl.pallas_call(fetch_kernel, out_shape=(shape((HEAD, CELLS), BF16), shape...]
    unnamed x6 -> x0, local copies, waits for them, and re-layouts: 1.33 us -> none
    pallas_call x1, Pallas kernels: 1.62 us -> 0.77 us  [body(): pl.pallas_call(select_kernel, out_shape=shape((N_TILE, ROWS, CAP * SB), B...]
    pallas_call x1, Pallas kernels: 4.14 us -> 4.79 us  [body(): pl.pallas_call(remap_kernel, out_shape=(shape((ROWS - WINDS, CELLS), BF16...]
  transfers between devices with their start and end apart: 1 -> 0, of which waited for: 1 -> 0; matrix products, arithmetic and copies ran while one was open for 0% -> 0% of each run, Pallas kernels for 3% -> 0%
where the time goes in v3:
time: 62 us; the launch traced here: 61.8 us
  blocking collectives  52.5 us (85%)
  Pallas kernels  8.7 us (14%)
  between operations  0.66 us (1%)
    all_to_all x1, blocking collectives, body(): packets = lax.all_to_all(packets, ('tile', 'face'), 0, 0, tiled=True)  18.9 us
    all_to_all x1, blocking collectives, body(): blocks = lax.all_to_all(blocks, 'tile', 0, 0, tiled=True)  17.5 us
    all_to_all x1, blocking collectives, body(): lax.all_to_all(asked, 'tile', 0, 0, tiled=True).reshape(N_TILE, LANES)  16.1 us
    pallas_call x1, Pallas kernels, body(): pl.pallas_call(remap_kernel, out_shape=(shape((ROWS - WINDS, CELLS), BF16...  4.79 us
    pallas_call x1, Pallas kernels, body(): pl.pallas_call(smooth_kernel, out_shape=(shape((ROWS - WINDS, CELLS), BF1...  2.18 us

profile of v3, /device:TPU:1, one launch (start us, length us, event | category | flops | bytes accessed | tf_op | source)
XLA Modules:
  0.0 61.8 jit_solution(6544981689899479240)
XLA Ops:
  0.6 1.0 %ask.1 = (s32[16,1,128]{2,1,0:T(1,128)S(1)}, s32[8,128]{1,0:T(8,128)S(1)}, bf16[48,2048]{1,0:T(8,128)(2,1)S(1)}) custom-call(s32[16]{0:T(128)} %bitcast.12, s32[3,1,4]{2,1,0:T(1,128)} %bitcast.11, bf16[48,2048]{1,0:T(8,128)(2,1)} %checkpoint_ref.1), custom_call_target="tpu_custom_call" | custom-call | tf_op jit(solution)/shard_map/ask/pallas_call | solution.py:395
  1.6 16.1 %all_to_all.15 = s32[16,1,128]{2,1,0:T(1,128)S(1)} all-to-all(s32[16,1,128]{2,1,0:T(1,128)S(1)} %get-tuple-element.15), channel_id=1, replica_groups=mesh['face'=8,'tile'=16] {'tile'}, dimensions={0} | all-to-all | bytes 16384 | tf_op jit(solution)/shard_map/all_to_all | solution.py:412
  17.7 0.8 %select.1 = bf16[16,48,512]{2,1,0:T(8,128)(2,1)S(1)} custom-call(s32[16,128]{1,0:T(8,128)S(1)} %bitcast.8, bf16[48,2048]{1,0:T(8,128)(2,1)S(1)} %get-tuple-element.16.held_ref), custom_call_target="tpu_custom_call" | custom-call | tf_op jit(solution)/shard_map/select/pallas_call | solution.py:413
  18.4 17.5 %all_to_all.16.blocks_ref = bf16[16,48,512]{2,1,0:T(8,128)(2,1)S(1)} all-to-all(bf16[16,48,512]{2,1,0:T(8,128)(2,1)S(1)} %select.1), channel_id=1, replica_groups=mesh['face'=8,'tile'=16] {'tile'}, dimensions={0} | all-to-all | bytes 1572864 | tf_op jit(solution)/shard_map/all_to_all | solution.py:421
  35.9 4.8 %remap.1 = (bf16[32,1024]{1,0:T(8,128)(2,1)S(1)}, f32[16,1024]{1,0:T(8,128)S(1)}, f32[8,1024]{1,0:T(8,128)S(1)}, bf16[128,1024]{1,0:T(8,128)(2,1)S(1)}, bf16[128,16,128]{2,1,0:T(8,128)(2,1)S(1)}) custom-call(s32[8,128]{1,0:T(8,128)S(1)} %get-tuple-element.14.meta_ref, bf16[16,48,512]{2,1,0:T(8,128)(2,1)S(1)} %all_to_all.16.blocks_ref, ...), custom_call_target="tpu_custom_call" | custom-call | flops 402653184 | bytes 9437184 | tf_op jit(solution)/shard_map/remap/pallas_call | solution.py:423
  40.7 18.9 %all_to_all.17.packets_ref = bf16[128,16,128]{2,1,0:T(8,128)(2,1)S(1)} all-to-all(bf16[128,16,128]{2,1,0:T(8,128)(2,1)S(1)} %get-tuple-element.17), channel_id=1, replica_groups=mesh['face'=8,'tile'=16] {'tile','face'}, dimensions={0} | all-to-all | bytes 1048576 | tf_op jit(solution)/shard_map/all_to_all | solution.py:445
  59.6 2.2 %smooth.1 = (bf16[32,1024]{1,0:T(8,128)(2,1)}, bf16[16,1024]{1,0:T(8,128)(2,1)}, f32[8,1024]{1,0:T(8,128)}) custom-call(s32[8,128]{1,0:T(8,128)S(1)} %get-tuple-element.14.meta_ref, bf16[128,16,128]{2,1,0:T(8,128)(2,1)S(1)} %all_to_all.17.packets_ref, f32[16,1024]{1,0:T(8,128)S(1)} %get-tuple-element.18.wind_ref, f32[8,1024]{1,0:T(8,128)S(1)} %get-tuple-element.19.trig_ref, ...), custom_call_target="tpu_custom_call" | custom-call | tf_op jit(solution)/shard_map/smooth/pallas_call | solution.py:447

commit v4 on v3

--- a/solution.py
+++ b/solution.py
@@ -107,9 +107,10 @@
 
 
 def select_kernel(asked_ref, held_ref, out_ref):
+    asked = asked_ref[...]
     for g in range(N_TILE):
         for j in range(CAP):
-            block = asked_ref[g, j] & (BLK_DEV - 1)
+            block = asked[g, j] & (BLK_DEV - 1)
             out_ref[g, :, j * SB : (j + 1) * SB] = held_ref[:, pl.ds(pl.multiple_of(block * SB, SB), SB)]
 
 
@@ -127,8 +128,9 @@
     ]
     for copy in copies:
         copy.start()
+    meta = meta_ref[...]
     for m in range(GROUPS):
-        chosen[:, CAP * SB * m : CAP * SB * (m + 1)] = blocks_ref[meta_ref[0, m]]
+        chosen[:, CAP * SB * m : CAP * SB * (m + 1)] = blocks_ref[meta[0, m]]
     total = None
 
     angle_copy.wait()
@@ -150,7 +152,7 @@
 
     line = iota((LANES, 1), 0)
     line_edge, line_at = line >> 5, line & 31
-    flipped = lane_pick(line_edge, [meta_ref[3, e] for e in range(4)]) == 1
+    flipped = lane_pick(line_edge, [meta[3, e] for e in range(4)]) == 1
     line_at = jnp.where(flipped, TS - 1 - line_at, line_at)
     rim_cell = jnp.where(
         line_edge == 0, (TS - 1) * TS + line_at,
@@ -184,8 +186,8 @@
     corners = got[:, 2 * LANES :]
     common_top = jnp.where((level == 5) | (level == 6), corners[24:32], 0.0)
     for e in range(4):
-        tile = meta_ref[1, e].astype(F32)
-        code = (meta_ref[2, e] * 2 + meta_ref[3, e]).astype(F32)
+        tile = meta[1, e].astype(F32)
+        code = (meta[2, e] * 2 + meta[3, e]).astype(F32)
         common_top = jnp.where((level == 4) & (lane == 96 + e), tile, common_top)
         common_top = jnp.where((level == 4) & (lane == 100 + e), code, common_top)
     common_low = jnp.where(
@@ -207,12 +209,14 @@
             group == 0, rim[8:16],
             jnp.where(group == 1, roll(rim[40:48], 32), jnp.where(group == 2, roll(rim[16:24], 32), common_low)),
         )
-        send_ref[slot(meta_ref[1, e])] = jnp.concatenate([top, low], axis=0).astype(BF16)
+        send_ref[slot(meta[1, e])] = jnp.concatenate([top, low], axis=0).astype(BF16)
 
 
 def smooth_kernel(
     meta_ref, packets_ref, wind_ref, trig_ref, place_ref, scalars_ref, scalars_out_ref, dgrid_ref, vortex_ref
 ):
+    meta = meta_ref[...]
+
     def packet(tile):
         both = packets_ref[slot(tile)].astype(F32)
         return both[:LEV], both[LEV:]
@@ -225,8 +229,8 @@
     group = lane >> 5
     at = lane & 31
     zero = jnp.zeros((LEV, LANES), F32)
-    edges = [meta_ref[2, e] for e in range(4)]
-    near = [packet(meta_ref[1, e]) for e in range(4)]
+    edges = [meta[2, e] for e in range(4)]
+    near = [packet(meta[1, e]) for e in range(4)]
 
     def code_of(top, edge):
         codes = pltpu.roll(top * 8.0 + roll(top, -4), (LANES - 96 - edge) & 127, 1)
@@ -365,16 +369,8 @@
     return pl.BlockSpec(memory_space=pltpu.VMEM)
 
 
-def smem():
-    return pl.BlockSpec(memory_space=pltpu.SMEM)
-
-
 def shape(dims, kind):
     return jax.ShapeDtypeStruct(dims, kind)
-
-
-def anywhere():
-    return pl.BlockSpec(memory_space=pl.ANY)
 
 
 def hbm():
@@ -413,7 +409,7 @@
     blocks = pl.pallas_call(
         select_kernel,
         out_shape=shape((N_TILE, ROWS, CAP * SB), BF16),
-        in_specs=[smem(), vmem()],
+        in_specs=[vmem(), vmem()],
         out_specs=vmem(),
         compiler_params=limit,
         name="select",
@@ -429,7 +425,7 @@
             shape((LANES, CELLS), BF16),
             shape((TILES, 16, LANES), BF16),
         ),
-        in_specs=[smem(), vmem(), hbm(), hbm()],
+        in_specs=[vmem(), vmem(), hbm(), hbm()],
         out_specs=(vmem(),) * 5,
         scratch_shapes=[
             pltpu.VMEM((ROWS, K * SB), BF16),
@@ -451,7 +447,7 @@
             shape((WINDS, CELLS), BF16),
             shape((LEV, CELLS), F32),
         ),
-        in_specs=[smem()] + [vmem()] * 5,
+        in_specs=[vmem()] * 6,
         out_specs=(vmem(),) * 3,
         compiler_params=limit,
         name="smooth",

time: 62 us -> 60.4 us (0.974)
  Pallas kernels: 8.7 us -> 7.05 us
where the time goes in v4:
time: 60.4 us; the launch traced here: 60.2 us
  blocking collectives  52.5 us (87%)
  Pallas kernels  7.05 us (12%)
  between operations  0.66 us (1%)
    all_to_all x1, blocking collectives, body(): packets = lax.all_to_all(packets, ('tile', 'face'), 0, 0, tiled=True)  18.9 us
    all_to_all x1, blocking collectives, body(): blocks = lax.all_to_all(blocks, 'tile', 0, 0, tiled=True)  17.5 us
    all_to_all x1, blocking collectives, body(): lax.all_to_all(asked, 'tile', 0, 0, tiled=True).reshape(N_TILE, LANES)  16.1 us
    pallas_call x1, Pallas kernels, body(): pl.pallas_call(remap_kernel, out_shape=(shape((ROWS - WINDS, CELLS), BF16...  4.21 us
    pallas_call x1, Pallas kernels, body(): pl.pallas_call(smooth_kernel, out_shape=(shape((ROWS - WINDS, CELLS), BF1...  1.69 us

profile of v4, /device:TPU:1, one launch (start us, length us, event | category | flops | bytes accessed | tf_op | source)
XLA Modules:
  0.0 60.2 jit_solution(17426704983867053351)
XLA Ops:
  0.6 1.0 %ask.1 = (s32[16,1,128]{2,1,0:T(1,128)S(1)}, s32[8,128]{1,0:T(8,128)S(1)}, bf16[48,2048]{1,0:T(8,128)(2,1)S(1)}) custom-call(s32[16]{0:T(128)} %bitcast.12, s32[3,1,4]{2,1,0:T(1,128)} %bitcast.11, bf16[48,2048]{1,0:T(8,128)(2,1)} %checkpoint_ref.1), custom_call_target="tpu_custom_call" | custom-call | tf_op jit(solution)/shard_map/ask/pallas_call | solution.py:391
  1.6 16.1 %all_to_all.15 = s32[16,1,128]{2,1,0:T(1,128)S(1)} all-to-all(s32[16,1,128]{2,1,0:T(1,128)S(1)} %get-tuple-element.15), channel_id=1, replica_groups=mesh['face'=8,'tile'=16] {'tile'}, dimensions={0} | all-to-all | bytes 16384 | tf_op jit(solution)/shard_map/all_to_all | solution.py:408
  17.7 0.2 select.1
  17.9 17.5 %all_to_all.16.blocks_ref = bf16[16,48,512]{2,1,0:T(8,128)(2,1)S(1)} all-to-all(bf16[16,48,512]{2,1,0:T(8,128)(2,1)S(1)} %select.1), channel_id=1, replica_groups=mesh['face'=8,'tile'=16] {'tile'}, dimensions={0} | all-to-all | bytes 1572864 | tf_op jit(solution)/shard_map/all_to_all | solution.py:417
  35.3 4.2 %remap.1 = (bf16[32,1024]{1,0:T(8,128)(2,1)S(1)}, f32[16,1024]{1,0:T(8,128)S(1)}, f32[8,1024]{1,0:T(8,128)S(1)}, bf16[128,1024]{1,0:T(8,128)(2,1)S(1)}, bf16[128,16,128]{2,1,0:T(8,128)(2,1)S(1)}) custom-call(s32[8,128]{1,0:T(8,128)S(1)} %get-tuple-element.14.meta_ref, bf16[16,48,512]{2,1,0:T(8,128)(2,1)S(1)} %all_to_all.16.blocks_ref, ...), custom_call_target="tpu_custom_call" | custom-call | flops 402653184 | bytes 9437184 | tf_op jit(solution)/shard_map/remap/pallas_call | solution.py:419
  39.5 18.9 %all_to_all.17.packets_ref = bf16[128,16,128]{2,1,0:T(8,128)(2,1)S(1)} all-to-all(bf16[128,16,128]{2,1,0:T(8,128)(2,1)S(1)} %get-tuple-element.17), channel_id=1, replica_groups=mesh['face'=8,'tile'=16] {'tile','face'}, dimensions={0} | all-to-all | bytes 1048576 | tf_op jit(solution)/shard_map/all_to_all | solution.py:441
  58.5 1.7 %smooth.1 = (bf16[32,1024]{1,0:T(8,128)(2,1)}, bf16[16,1024]{1,0:T(8,128)(2,1)}, f32[8,1024]{1,0:T(8,128)}) custom-call(s32[8,128]{1,0:T(8,128)S(1)} %get-tuple-element.14.meta_ref, bf16[128,16,128]{2,1,0:T(8,128)(2,1)S(1)} %all_to_all.17.packets_ref, f32[16,1024]{1,0:T(8,128)S(1)} %get-tuple-element.18.wind_ref, f32[8,1024]{1,0:T(8,128)S(1)} %get-tuple-element.19.trig_ref, ...), custom_call_target="tpu_custom_call" | custom-call | tf_op jit(solution)/shard_map/smooth/pallas_call | solution.py:443

commit v5 on v4

--- a/solution.py
+++ b/solution.py
@@ -136,19 +136,16 @@
     angle_copy.wait()
     trig_ref[...] = jnp.where((iota((LEV, CELLS), 0) & 1) == 0, jnp.cos(angle[...]), jnp.sin(angle[...]))
 
-    lane = iota((1, 3 * LANES), 1)
-    edge, depth, at = (lane >> 6) & 3, (lane >> 5) & 1, lane & 31
-    rim_cell = jnp.where(
-        edge == 0, (TS - 1 - depth) * TS + at,
-        jnp.where(edge == 1, at * TS + TS - 1 - depth, jnp.where(edge == 2, depth * TS + at, at * TS + depth)),
-    )
+    lane = iota((1, 2 * LANES), 1)
+    depth, at = (lane >> 5) & 1, lane & 31
+    column_cell = at * TS + jnp.where((lane >> 6) == 0, TS - 1 - depth, depth)
     corner, k = (lane >> 2) & 3, lane & 3
     c_row, c_col = (corner >> 1) * (TS - 1), (corner & 1) * (TS - 1)
     c_row = jnp.where(k == 2, jnp.where(c_row == 0, 1, TS - 2), c_row)
     c_col = jnp.where(k == 1, jnp.where(c_col == 0, 1, TS - 2), c_col)
     corner_cell = jnp.where((lane & 127) >= 96, c_row * TS + c_col, -1)
-    taken = jnp.where(lane < 2 * LANES, rim_cell, corner_cell)
-    pick_ref[...] = (iota((CELLS, 3 * LANES), 0) == taken).astype(F32).astype(BF16)
+    taken = jnp.where(lane < LANES, column_cell, corner_cell)
+    pick_ref[...] = (iota((CELLS, 2 * LANES), 0) == taken).astype(F32).astype(BF16)
 
     line = iota((LANES, 1), 0)
     line_edge, line_at = line >> 5, line & 31
@@ -178,12 +175,13 @@
     curl = cosine * (0.5 * (nx - nxm) - 0.5 * (ey - eym)) - sine * (0.5 * (ex - exm) + 0.5 * (ny - nym))
 
     hi, lo = halves(jnp.concatenate([east, north, curl, trig], axis=0))
-    got = dot(jnp.concatenate([hi, lo], axis=0).astype(BF16), pick_ref[...])
+    both = jnp.concatenate([hi, lo], axis=0)
+    got = dot(both.astype(BF16), pick_ref[...])
 
     lane = iota((LEV, LANES), 1)
     level = iota((LEV, LANES), 0)
     group = lane >> 5
-    corners = got[:, 2 * LANES :]
+    corners = got[:, LANES:]
     common_top = jnp.where((level == 5) | (level == 6), corners[24:32], 0.0)
     for e in range(4):
         tile = meta[1, e].astype(F32)
@@ -197,18 +195,25 @@
     common = jnp.concatenate([common_top, common_low], axis=0).astype(BF16)
     for t in range(TILES):
         send_ref[t] = common
-    for e in range(4):
-        rim = roll(got[:, LANES * (e // 2) : LANES * (e // 2 + 1)], -64 * (e % 2))
-        top = jnp.where(
-            group == 0, rim[0:8],
-            jnp.where(group == 1, roll(rim[32:40], 32), jnp.where(group == 2, roll(rim[16:24], 64), common_top)),
-        )
-        top = jnp.where((group == 3) & (level < 2), roll(rim[24:32], 96), top)
-        top = jnp.where((group == 3) & ((level == 2) | (level == 3)), roll(rim[24:32], 64), top)
-        low = jnp.where(
-            group == 0, rim[8:16],
-            jnp.where(group == 1, roll(rim[40:48], 32), jnp.where(group == 2, roll(rim[16:24], 32), common_low)),
-        )
+    sources = [
+        (both[:, CELLS - LANES :], 96, 64),
+        (got[:, :LANES], 0, 32),
+        (both[:, :LANES], 0, 32),
+        (got[:, :LANES], 64, 96),
+    ]
+    for e, (rim, at0, at1) in enumerate(sources):
+
+        def to(goal, rows, start):
+            return rim[rows] if goal == start else roll(rim[rows], goal - start)
+
+        east_rows, north_rows, curl_rows, trig_rows = (slice(8 * i, 8 * i + 8) for i in range(4))
+        east_low, north_low = slice(32, 40), slice(40, 48)
+        top = jnp.where(group == 2, to(64, curl_rows, at0), common_top)
+        top = jnp.where(group == 0, to(0, east_rows, at0), jnp.where(group == 1, to(32, east_low, at0), top))
+        top = jnp.where((group == 3) & (level < 2), to(96, trig_rows, at0), top)
+        top = jnp.where((group == 3) & ((level == 2) | (level == 3)), to(96, trig_rows, at1), top)
+        low = jnp.where(group == 2, to(64, curl_rows, at1), common_low)
+        low = jnp.where(group == 0, to(0, north_rows, at0), jnp.where(group == 1, to(32, north_low, at0), low))
         send_ref[slot(meta[1, e])] = jnp.concatenate([top, low], axis=0).astype(BF16)
 
 
@@ -348,9 +353,8 @@
     after = jnp.where(at == 31, far_c, roll(c0, -1))
     before = jnp.where(at == 0, far_c, roll(c0, 1))
     s0 = c0 + 0.2 * (c1 + after + before - 4.0 * c0)
-    halo_e, halo_n, halo_c, halo_s = placed(
-        [(east_hi, east_lo), (north_hi, north_lo), halves(c0), halves(s0)]
-    )
+    halo_e, halo_n = placed([(east_hi, east_lo), (north_hi, north_lo)])
+    halo_c, halo_s = placed([halves(c0), halves(s0)])
 
     ex, exm, ey, eym = shifts(east, halo_e)
     nx, nxm, ny, nym = shifts(north, halo_n)
@@ -430,7 +434,7 @@
         scratch_shapes=[
             pltpu.VMEM((ROWS, K * SB), BF16),
             pltpu.VMEM((K * SB, CELLS), BF16),
-            pltpu.VMEM((CELLS, 3 * LANES), BF16),
+            pltpu.VMEM((CELLS, 2 * LANES), BF16),
             pltpu.VMEM((1, CELLS), F32),
             pltpu.SemaphoreType.DMA((K * SB // CHUNK + 1,)),
         ],

time: 60.4 us -> 60.2 us (level)
  no operation moved by 1% of the time
where the time goes in v5:
time: 60.2 us; the launch traced here: 60 us
  blocking collectives  52.5 us (87%)
  Pallas kernels  6.83 us (11%)
  between operations  0.66 us (1%)
    all_to_all x1, blocking collectives, body(): packets = lax.all_to_all(packets, ('tile', 'face'), 0, 0, tiled=True)  18.9 us
    all_to_all x1, blocking collectives, body(): blocks = lax.all_to_all(blocks, 'tile', 0, 0, tiled=True)  17.5 us
    all_to_all x1, blocking collectives, body(): lax.all_to_all(asked, 'tile', 0, 0, tiled=True).reshape(N_TILE, LANES)  16.1 us
    pallas_call x1, Pallas kernels, body(): pl.pallas_call(remap_kernel, out_shape=(shape((ROWS - WINDS, CELLS), BF16...  4.11 us
    pallas_call x1, Pallas kernels, body(): pl.pallas_call(smooth_kernel, out_shape=(shape((ROWS - WINDS, CELLS), BF1...  1.57 us

profile of v5, /device:TPU:1, one launch (start us, length us, event | category | flops | bytes accessed | tf_op | source)
XLA Modules:
  0.0 60.0 jit_solution(17760452989895242048)
XLA Ops:
  0.6 1.0 %ask.1 = (s32[16,1,128]{2,1,0:T(1,128)S(1)}, s32[8,128]{1,0:T(8,128)S(1)}, bf16[48,2048]{1,0:T(8,128)(2,1)S(1)}) custom-call(s32[16]{0:T(128)} %bitcast.12, s32[3,1,4]{2,1,0:T(1,128)} %bitcast.11, bf16[48,2048]{1,0:T(8,128)(2,1)} %checkpoint_ref.1), custom_call_target="tpu_custom_call" | custom-call | tf_op jit(solution)/shard_map/ask/pallas_call | solution.py:395
  1.6 16.1 %all_to_all.15 = s32[16,1,128]{2,1,0:T(1,128)S(1)} all-to-all(s32[16,1,128]{2,1,0:T(1,128)S(1)} %get-tuple-element.15), channel_id=1, replica_groups=mesh['face'=8,'tile'=16] {'tile'}, dimensions={0} | all-to-all | bytes 16384 | tf_op jit(solution)/shard_map/all_to_all | solution.py:412
  17.7 0.2 select.1
  17.9 17.5 %all_to_all.16.blocks_ref = bf16[16,48,512]{2,1,0:T(8,128)(2,1)S(1)} all-to-all(bf16[16,48,512]{2,1,0:T(8,128)(2,1)S(1)} %select.1), channel_id=1, replica_groups=mesh['face'=8,'tile'=16] {'tile'}, dimensions={0} | all-to-all | bytes 1572864 | tf_op jit(solution)/shard_map/all_to_all | solution.py:421
  35.3 4.1 %remap.1 = (bf16[32,1024]{1,0:T(8,128)(2,1)S(1)}, f32[16,1024]{1,0:T(8,128)S(1)}, f32[8,1024]{1,0:T(8,128)S(1)}, bf16[128,1024]{1,0:T(8,128)(2,1)S(1)}, bf16[128,16,128]{2,1,0:T(8,128)(2,1)S(1)}) custom-call(s32[8,128]{1,0:T(8,128)S(1)} %get-tuple-element.14.meta_ref, bf16[16,48,512]{2,1,0:T(8,128)(2,1)S(1)} %all_to_all.16.blocks_ref, ...), custom_call_target="tpu_custom_call" | custom-call | flops 402653184 | bytes 9437184 | tf_op jit(solution)/shard_map/remap/pallas_call | solution.py:423
  39.4 18.9 %all_to_all.17.packets_ref = bf16[128,16,128]{2,1,0:T(8,128)(2,1)S(1)} all-to-all(bf16[128,16,128]{2,1,0:T(8,128)(2,1)S(1)} %get-tuple-element.17), channel_id=1, replica_groups=mesh['face'=8,'tile'=16] {'tile','face'}, dimensions={0} | all-to-all | bytes 1048576 | tf_op jit(solution)/shard_map/all_to_all | solution.py:445
  58.4 1.6 %smooth.1 = (bf16[32,1024]{1,0:T(8,128)(2,1)}, bf16[16,1024]{1,0:T(8,128)(2,1)}, f32[8,1024]{1,0:T(8,128)}) custom-call(s32[8,128]{1,0:T(8,128)S(1)} %get-tuple-element.14.meta_ref, bf16[128,16,128]{2,1,0:T(8,128)(2,1)S(1)} %all_to_all.17.packets_ref, f32[16,1024]{1,0:T(8,128)S(1)} %get-tuple-element.18.wind_ref, f32[8,1024]{1,0:T(8,128)S(1)} %get-tuple-element.19.trig_ref, ...), custom_call_target="tpu_custom_call" | custom-call | tf_op jit(solution)/shard_map/smooth/pallas_call | solution.py:447

commit v6 on v5

--- a/solution.py
+++ b/solution.py
@@ -101,9 +101,13 @@
     copies[2].wait()
 
 
+def slot_bits(tile):
+    y, z = (tile >> 4) & 3, (tile >> 1) & 3
+    return (y << 5) | (z << 3) | ((tile >> 6) << 2) | (((tile >> 3) & 1) << 1) | (tile & 1)
+
+
 def slot(tile):
-    tile = jnp.clip(tile, 0, TILES - 1)
-    return (tile & (N_TILE - 1)) * (TILES // N_TILE) + (tile >> 4)
+    return slot_bits(jnp.clip(tile, 0, TILES - 1))
 
 
 def select_kernel(asked_ref, held_ref, out_ref):
@@ -442,7 +446,9 @@
         cost_estimate=cost(2 * ROWS * K * SB * CELLS, 9 * MIB),
         name="remap",
     )(meta, blocks, in_hbm(weights), in_hbm(rotation_angle[0, 0].reshape(1, CELLS)))
-    packets = lax.all_to_all(packets, ("tile", "face"), 0, 0, tiled=True)
+    packets = lax.all_to_all(
+        packets, ("face", "tile"), 0, 0, axis_index_groups=[sorted(range(TILES), key=slot_bits)], tiled=True
+    )
 
     scalars, dgrid, vortex = pl.pallas_call(
         smooth_kernel,

time: 60.2 us -> 60.5 us (level)
  no operation moved by 1% of the time
where the time goes in v6:
time: 60.5 us; the launch traced here: 60.3 us
  blocking collectives  52.8 us (87%)
  Pallas kernels  6.89 us (11%)
  between operations  0.66 us (1%)
    all_to_all x1, blocking collectives, body(): lax.all_to_all(packets, ('face', 'tile'), 0, 0, axis_index_groups=[sorted...  19.2 us
    all_to_all x1, blocking collectives, body(): blocks = lax.all_to_all(blocks, 'tile', 0, 0, tiled=True)  17.5 us
    all_to_all x1, blocking collectives, body(): lax.all_to_all(asked, 'tile', 0, 0, tiled=True).reshape(N_TILE, LANES)  16.1 us
    pallas_call x1, Pallas kernels, body(): pl.pallas_call(remap_kernel, out_shape=(shape((ROWS - WINDS, CELLS), BF16...  4.11 us
    pallas_call x1, Pallas kernels, body(): pl.pallas_call(smooth_kernel, out_shape=(shape((ROWS - WINDS, CELLS), BF1...  1.63 us

profile of v6, /device:TPU:1, one launch (start us, length us, event | category | flops | bytes accessed | tf_op | source)
XLA Modules:
  0.0 60.3 jit_solution(7814985189159961051)
XLA Ops:
  0.6 1.0 %ask.1 = (s32[16,1,128]{2,1,0:T(1,128)S(1)}, s32[8,128]{1,0:T(8,128)S(1)}, bf16[48,2048]{1,0:T(8,128)(2,1)S(1)}) custom-call(s32[16]{0:T(128)} %bitcast.12, s32[3,1,4]{2,1,0:T(1,128)} %bitcast.11, bf16[48,2048]{1,0:T(8,128)(2,1)} %checkpoint_ref.1), custom_call_target="tpu_custom_call" | custom-call | tf_op jit(solution)/shard_map/ask/pallas_call | solution.py:399
  1.6 16.1 %all_to_all.15 = s32[16,1,128]{2,1,0:T(1,128)S(1)} all-to-all(s32[16,1,128]{2,1,0:T(1,128)S(1)} %get-tuple-element.15), channel_id=1, replica_groups=mesh['face'=8,'tile'=16] {'tile'}, dimensions={0} | all-to-all | bytes 16384 | tf_op jit(solution)/shard_map/all_to_all | solution.py:416
  17.7 0.2 select.1
  17.9 17.5 %all_to_all.16.blocks_ref = bf16[16,48,512]{2,1,0:T(8,128)(2,1)S(1)} all-to-all(bf16[16,48,512]{2,1,0:T(8,128)(2,1)S(1)} %select.1), channel_id=1, replica_groups=mesh['face'=8,'tile'=16] {'tile'}, dimensions={0} | all-to-all | bytes 1572864 | tf_op jit(solution)/shard_map/all_to_all | solution.py:425
  35.3 4.1 %remap.1 = (bf16[32,1024]{1,0:T(8,128)(2,1)S(1)}, f32[16,1024]{1,0:T(8,128)S(1)}, f32[8,1024]{1,0:T(8,128)S(1)}, bf16[128,1024]{1,0:T(8,128)(2,1)S(1)}, bf16[128,16,128]{2,1,0:T(8,128)(2,1)S(1)}) custom-call(s32[8,128]{1,0:T(8,128)S(1)} %get-tuple-element.14.meta_ref, bf16[16,48,512]{2,1,0:T(8,128)(2,1)S(1)} %all_to_all.16.blocks_ref, ...), custom_call_target="tpu_custom_call" | custom-call | flops 402653184 | bytes 9437184 | tf_op jit(solution)/shard_map/remap/pallas_call | solution.py:427
  39.4 19.2 %all_to_all.17.packets_ref = bf16[128,16,128]{2,1,0:T(8,128)(2,1)S(1)} all-to-all(bf16[128,16,128]{2,1,0:T(8,128)(2,1)S(1)} %get-tuple-element.17), channel_id=1, replica_groups={{0,1,8,9,64,65,72,73,2,3,10,11,66,67,74,75,4,5,12,13,68,69,76,77,6,7,14..., dimensions={0} | all-to-all | bytes 1048576 | tf_op jit(solution)/shard_map/all_to_all | solution.py:449
  58.7 1.6 %smooth.1 = (bf16[32,1024]{1,0:T(8,128)(2,1)}, bf16[16,1024]{1,0:T(8,128)(2,1)}, f32[8,1024]{1,0:T(8,128)}) custom-call(s32[8,128]{1,0:T(8,128)S(1)} %get-tuple-element.14.meta_ref, bf16[128,16,128]{2,1,0:T(8,128)(2,1)S(1)} %all_to_all.17.packets_ref, f32[16,1024]{1,0:T(8,128)S(1)} %get-tuple-element.18.wind_ref, f32[8,1024]{1,0:T(8,128)S(1)} %get-tuple-element.19.trig_ref, ...), custom_call_target="tpu_custom_call" | custom-call | tf_op jit(solution)/shard_map/smooth/pallas_call | solution.py:453

commit v7 on v5

--- a/solution.py
+++ b/solution.py
@@ -354,7 +354,8 @@
     before = jnp.where(at == 0, far_c, roll(c0, 1))
     s0 = c0 + 0.2 * (c1 + after + before - 4.0 * c0)
     halo_e, halo_n = placed([(east_hi, east_lo), (north_hi, north_lo)])
-    halo_c, halo_s = placed([halves(c0), halves(s0)])
+    (halo_c,) = placed([halves(c0)])
+    (halo_s,) = placed([halves(s0)])
 
     ex, exm, ey, eym = shifts(east, halo_e)
     nx, nxm, ny, nym = shifts(north, halo_n)

time: 60.2 us -> 60.2 us (level)
  no operation moved by 1% of the time
where the time goes in v7:
time: 60.2 us; the launch traced here: 60 us
  blocking collectives  52.5 us (87%)
  Pallas kernels  6.87 us (11%)
  between operations  0.66 us (1%)
    all_to_all x1, blocking collectives, body(): packets = lax.all_to_all(packets, ('tile', 'face'), 0, 0, tiled=True)  18.9 us
    all_to_all x1, blocking collectives, body(): blocks = lax.all_to_all(blocks, 'tile', 0, 0, tiled=True)  17.5 us
    all_to_all x1, blocking collectives, body(): lax.all_to_all(asked, 'tile', 0, 0, tiled=True).reshape(N_TILE, LANES)  16.1 us
    pallas_call x1, Pallas kernels, body(): pl.pallas_call(remap_kernel, out_shape=(shape((ROWS - WINDS, CELLS), BF16...  4.11 us
    pallas_call x1, Pallas kernels, body(): pl.pallas_call(smooth_kernel, out_shape=(shape((ROWS - WINDS, CELLS), BF1...  1.6 us

profile of v7, /device:TPU:1, one launch (start us, length us, event | category | flops | bytes accessed | tf_op | source)
XLA Modules:
  0.0 60.0 jit_solution(5661351099514099085)
XLA Ops:
  0.6 1.0 %ask.1 = (s32[16,1,128]{2,1,0:T(1,128)S(1)}, s32[8,128]{1,0:T(8,128)S(1)}, bf16[48,2048]{1,0:T(8,128)(2,1)S(1)}) custom-call(s32[16]{0:T(128)} %bitcast.12, s32[3,1,4]{2,1,0:T(1,128)} %bitcast.11, bf16[48,2048]{1,0:T(8,128)(2,1)} %checkpoint_ref.1), custom_call_target="tpu_custom_call" | custom-call | tf_op jit(solution)/shard_map/ask/pallas_call | solution.py:396
  1.6 16.1 %all_to_all.15 = s32[16,1,128]{2,1,0:T(1,128)S(1)} all-to-all(s32[16,1,128]{2,1,0:T(1,128)S(1)} %get-tuple-element.15), channel_id=1, replica_groups=mesh['face'=8,'tile'=16] {'tile'}, dimensions={0} | all-to-all | bytes 16384 | tf_op jit(solution)/shard_map/all_to_all | solution.py:413
  17.7 0.2 select.1
  17.9 17.5 %all_to_all.16.blocks_ref = bf16[16,48,512]{2,1,0:T(8,128)(2,1)S(1)} all-to-all(bf16[16,48,512]{2,1,0:T(8,128)(2,1)S(1)} %select.1), channel_id=1, replica_groups=mesh['face'=8,'tile'=16] {'tile'}, dimensions={0} | all-to-all | bytes 1572864 | tf_op jit(solution)/shard_map/all_to_all | solution.py:422
  35.3 4.1 %remap.1 = (bf16[32,1024]{1,0:T(8,128)(2,1)S(1)}, f32[16,1024]{1,0:T(8,128)S(1)}, f32[8,1024]{1,0:T(8,128)S(1)}, bf16[128,1024]{1,0:T(8,128)(2,1)S(1)}, bf16[128,16,128]{2,1,0:T(8,128)(2,1)S(1)}) custom-call(s32[8,128]{1,0:T(8,128)S(1)} %get-tuple-element.14.meta_ref, bf16[16,48,512]{2,1,0:T(8,128)(2,1)S(1)} %all_to_all.16.blocks_ref, ...), custom_call_target="tpu_custom_call" | custom-call | flops 402653184 | bytes 9437184 | tf_op jit(solution)/shard_map/remap/pallas_call | solution.py:424
  39.4 18.9 %all_to_all.17.packets_ref = bf16[128,16,128]{2,1,0:T(8,128)(2,1)S(1)} all-to-all(bf16[128,16,128]{2,1,0:T(8,128)(2,1)S(1)} %get-tuple-element.17), channel_id=1, replica_groups=mesh['face'=8,'tile'=16] {'tile','face'}, dimensions={0} | all-to-all | bytes 1048576 | tf_op jit(solution)/shard_map/all_to_all | solution.py:446
  58.4 1.6 %smooth.1 = (bf16[32,1024]{1,0:T(8,128)(2,1)}, bf16[16,1024]{1,0:T(8,128)(2,1)}, f32[8,1024]{1,0:T(8,128)}) custom-call(s32[8,128]{1,0:T(8,128)S(1)} %get-tuple-element.14.meta_ref, bf16[128,16,128]{2,1,0:T(8,128)(2,1)S(1)} %all_to_all.17.packets_ref, f32[16,1024]{1,0:T(8,128)S(1)} %get-tuple-element.18.wind_ref, f32[8,1024]{1,0:T(8,128)S(1)} %get-tuple-element.19.trig_ref, ...), custom_call_target="tpu_custom_call" | custom-call | tf_op jit(solution)/shard_map/smooth/pallas_call | solution.py:448
